TPU v7x, 512 devices: a whole 4x8x8 slice. The times are simulated.
512 devices in a mesh: row: 32 (over y, z_lo, core), col: 16 (over z_hi, x).
Axes of the slice: x: 4, y: 8, z: 8 (z_hi: 4, z_lo: 2; z = z_hi * 2 + z_lo), core: 2. Of those that a mesh axis runs over, the one named last changes fastest.
Arguments:
- modes: bfloat16 [3072, 1536, 128], P('row', 'col'), may hold values from -0.29882812 to 0.29882812
- conductivity: float32 [2560, 1280], P('row', 'col'), may hold values from 0.1 to 10
- storage: float32 [2560, 1280], P('row', 'col'), may hold values from 0.5 to 8
- owners: int32 [32, 16, 16, 1], P('row', 'col'), may hold values from 0 to 15; in each aligned block of 16 rows (0 to 15, 16 to 31, ..., all dimensions but the last counted through in order) at most 2 rows name the same one
Outputs:
- coarse_self: float32 [32, 512, 8, 128], P('row', 'col')
- coarse_cross: float32 [32, 512, 8, 8, 128], P('row', 'col')
Inputs may be any that keep to these rules, and one draw needn't show every extreme that they name: Among the 16 entries owners[r, c, :, 0] of one subdomain no column appears more than 2 times, and some column appears exactly 2 times in some subdomain.
All inputs are finite; a program needn't handle non-finite values.
Results may differ from a plain program's by a relative error of at most 0.0046.
Values may be sent and summed in bfloat16 or wider, within the bound.
A program may use at most 64 MiB of HBM per device.

v0:
```python
import math

import jax
import jax.numpy as jnp
from jax import lax
from jax.sharding import PartitionSpec as P

SWEEPS = 3
GROUPS = 16
SLOTS = 32


stencil_offsets = (
    (-1, -1, 0.5),
    (-1, 0, 1.0),
    (-1, 1, 0.5),
    (0, -1, 1.0),
    (0, 1, 1.0),
    (1, -1, 0.5),
    (1, 0, 1.0),
    (1, 1, 0.5),
)


def passed_along(block, axis, distance):
    devices = range(lax.axis_size(axis))
    route = [(i - distance, i) for i in devices if i - distance in devices]
    return lax.ppermute(block, axis, route)


def extended(block, sides, width):
    for axis, dim in sides:
        count = lax.axis_size(axis)
        forward = [(i, i + 1) for i in range(count - 1)]
        backward = [(target, source) for source, target in forward]
        low = lax.ppermute(
            lax.slice_in_dim(block, block.shape[dim] - width, None, axis=dim), axis, forward
        )
        high = lax.ppermute(lax.slice_in_dim(block, 0, width, axis=dim), axis, backward)
        block = jnp.concatenate([low, block, high], axis=dim)
    return block


def chebyshev_weights(count):
    return [
        1.0 / (1.15 + 0.85 * math.cos(math.pi * (2 * position + 1) / (2 * count)))
        for position in range(count)
    ]


def couplings(coefficient):
    size_a = coefficient.shape[0] - 2
    size_b = coefficient.shape[1] - 2
    center = coefficient[1 : size_a + 1, 1 : size_b + 1]
    result = []
    for shift_a, shift_b, factor in stencil_offsets:
        result.append(
            factor
            * 0.5
            * (
                center
                + coefficient[
                    1 + shift_a : size_a + 1 + shift_a, 1 + shift_b : size_b + 1 + shift_b
                ]
            )
        )
    return result


def apply_operator(source_field, weights, diagonal):
    size_a = diagonal.shape[0]
    size_b = diagonal.shape[1]
    accumulated = diagonal[:, :, None] * source_field[1 : size_a + 1, 1 : size_b + 1]
    for (shift_a, shift_b, factor), weight in zip(stencil_offsets, weights):
        accumulated = (
            accumulated
            - weight[:, :, None]
            * source_field[1 + shift_a : size_a + 1 + shift_a, 1 + shift_b : size_b + 1 + shift_b]
        )
    return accumulated


def smooth_and_apply(mode_tile, conduct_tile, storage_tile, inside_tile, sweep_count):
    weights_f = couplings(jnp.pad(conduct_tile, 1))
    diagonal_f = storage_tile + sum(weights_f)
    weights_e = [weight[1:-1, 1:-1] for weight in weights_f]
    diagonal_e = diagonal_f[1:-1, 1:-1]
    inside_e = inside_tile[1:-1, 1:-1]
    inverse = inside_e / (diagonal_e + 1.0 - inside_e)
    current = mode_tile.astype(jnp.float32) * inside_e[:, :, None]
    for omega in chebyshev_weights(sweep_count):
        applied = apply_operator(jnp.pad(current, ((1, 1), (1, 1), (0, 0))), weights_e, diagonal_e)
        current = current - omega * (inverse[:, :, None] * applied)
    smoothed = lax.optimization_barrier(current.astype(jnp.bfloat16))
    image = apply_operator(
        jnp.pad(smoothed.astype(jnp.float32), ((2, 2), (2, 2), (0, 0))), weights_f, diagonal_f
    )
    return (smoothed, image.astype(jnp.bfloat16))


def pair_block(first_tile, second_tile):
    first_flat = first_tile.reshape(-1, first_tile.shape[2])
    second_flat = second_tile.reshape(-1, second_tile.shape[2])
    return lax.dot_general(
        first_flat, second_flat, (((0,), (0,)), ((), ())), preferred_element_type=jnp.float32
    )


def mode_region(smoothed, pair_kind, cell_count, strip_width):
    extent = smoothed.shape[0]
    if pair_kind == 0:
        return smoothed[cell_count - 1 : extent, :]
    if pair_kind == 1:
        return smoothed[:, cell_count - 1 : extent]
    if pair_kind == 2:
        return smoothed[cell_count - 1 : extent, cell_count - 1 : extent]
    return smoothed[cell_count - 1 : extent, 0:strip_width]


def image_region(image, pair_kind, strip_width):
    full_size = image.shape[0]
    if pair_kind == 0:
        return image[0:strip_width, 1 : full_size - 1]
    if pair_kind == 1:
        return image[1 : full_size - 1, 0:strip_width]
    if pair_kind == 2:
        return image[0:strip_width, 0:strip_width]
    return image[0:strip_width, full_size - strip_width : full_size]


def fetch_pieces(pieces, sign):
    along_a, along_b, corner_ahead, corner_behind = pieces
    got_a = passed_along(along_a, "row", sign)
    got_b = passed_along(along_b, "col", sign)
    hop_ahead = passed_along(corner_ahead, "col", sign)
    hop_behind = passed_along(corner_behind, "col", -sign)
    got_ahead, got_behind = passed_along((hop_ahead, hop_behind), "row", sign)
    return (got_a, got_b, got_ahead, got_behind)


def return_blocks(blocks, sign):
    block_a, block_b, block_ahead, block_behind = blocks
    got_b, hop_ahead = passed_along((block_b, block_ahead), "col", sign)
    hop_behind = passed_along(block_behind.astype(jnp.bfloat16), "col", -sign).astype(
        block_behind.dtype
    )
    got_a, got_ahead, got_behind = passed_along((block_a, hop_ahead, hop_behind), "row", sign)
    return (got_a, got_b, got_ahead, got_behind)


def on_device(modes, conductivity, storage, owners):
    extent = modes.shape[0]
    cell_count = conductivity.shape[0]
    margin = (extent - cell_count) // 2 + 1
    full_size = extent + 2
    strip_width = extent - cell_count + 1
    mode_count = modes.shape[2]
    stacked = jnp.stack([conductivity, storage])
    widened = extended(stacked, (("row", 1), ("col", 2)), margin)
    position_a = (
        lax.axis_index("row") * cell_count - margin + jnp.arange(full_size, dtype=jnp.int32)
    )
    position_b = (
        lax.axis_index("col") * cell_count - margin + jnp.arange(full_size, dtype=jnp.int32)
    )
    inside_a = ((position_a >= 0) & (position_a < cell_count * lax.axis_size("row"))).astype(
        jnp.float32
    )
    inside_b = ((position_b >= 0) & (position_b < cell_count * lax.axis_size("col"))).astype(
        jnp.float32
    )
    inside_tile = inside_a[:, None] * inside_b[None, :]
    smoothed, image = smooth_and_apply(modes, widened[0], widened[1], inside_tile, SWEEPS)
    pieces = tuple((image_region(image, pair_kind, strip_width) for pair_kind in range(4)))
    arrived = fetch_pieces(pieces, -1)
    self_block = pair_block(smoothed, image[1:-1, 1:-1])
    formed = [
        pair_block(mode_region(smoothed, pair_kind, cell_count, strip_width), arrived[pair_kind])
        for pair_kind in range(4)
    ]
    lower_blocks = return_blocks(tuple((jnp.transpose(block) for block in formed)), 1)
    cross = jnp.stack(
        [
            lower_blocks[2],
            lower_blocks[0],
            lower_blocks[3],
            lower_blocks[1],
            formed[1],
            formed[3],
            formed[0],
            formed[2],
        ]
    )
    group_rows = mode_count // GROUPS
    self_groups = self_block.reshape(GROUPS, group_rows * mode_count)
    cross_groups = (
        cross.reshape(8, GROUPS, group_rows, mode_count)
        .transpose(1, 0, 2, 3)
        .reshape(GROUPS, 8 * group_rows * mode_count)
    )
    destination = owners.reshape(GROUPS)
    column_count = lax.axis_size("col")
    most_each = SLOTS // column_count
    chosen = (destination[:, None] == jnp.arange(column_count, dtype=jnp.int32)[None, :]).astype(
        jnp.int32
    )
    earlier = jnp.cumsum(chosen, axis=0) - chosen
    rank_in = jnp.sum(earlier * chosen, axis=1)
    slot_of = destination * most_each + rank_in
    placing = (slot_of[None, :] == jnp.arange(SLOTS, dtype=jnp.int32)[:, None]).astype(jnp.float32)
    send_self = jnp.dot(placing, self_groups, precision=lax.Precision.HIGHEST)
    send_cross = jnp.dot(placing, cross_groups, precision=lax.Precision.HIGHEST)
    got_self, got_cross = (
        lax.all_to_all(send_self, "col", split_axis=0, concat_axis=0, tiled=True),
        lax.all_to_all(send_cross, "col", split_axis=0, concat_axis=0, tiled=True),
    )
    return (
        got_self.reshape(1, SLOTS, group_rows, mode_count),
        got_cross.reshape(1, SLOTS, 8, group_rows, mode_count),
    )


def solution(mesh):
    return jax.shard_map(
        on_device,
        mesh=mesh,
        in_specs=(
            P("row", "col", None),
            P("row", "col"),
            P("row", "col"),
            P("row", "col", None, None),
        ),
        out_specs=(P("row", "col", None, None), P("row", "col", None, None, None)),
        check_vma=False,
    )
```

profile of v0, /device:TPU:96, one launch (start us, length us, event | category | flops | bytes accessed | tf_op | source)
XLA Modules:
  0.0 214.3 jit_solution(8596579852357436889)
XLA Ops:
  0.6 0.8 pad_maximum_fusion.3
  1.4 1.9 collective-permute-start
  3.3 3.6 %collective-permute-start.1 = (f32[2,9,80]{2,1,0:T(8,128)S(1)}, f32[2,9,80]{2,1,0:T(8,128)S(1)}, u32[]{:S(2)}, u32[]{:S(2)}) collective-permute-start(f32[2,9,80]{2,1,0:T(8,128)S(1)} %get-tuple-element.16), channel_id=1, source_target_pairs={{16,0},{32,16},{48,32},{64,48},{80,64},{96,80},{112,96},{128,112},... | collective-permute-start | bytes 17288 | tf_op jit(solution)/shard_map/ppermute | solution.py:39
  7.0 0.7 fusion.88
  7.7 0.8 select_reduce_fusion
  8.6 0.8 pad_maximum_fusion
  9.4 0.1 fusion.90
  9.5 3.4 %collective-permute-start.2 = (f32[2,98,9]{2,1,0:T(8,128)S(1)}, f32[2,98,9]{2,1,0:T(8,128)S(1)}, u32[]{:S(2)}, u32[]{:S(2)}) collective-permute-start(f32[2,98,9]{2,1,0:T(8,128)S(1)} %get-tuple-element.13), channel_id=1, source_target_pairs={{0,1},{1,2},{2,3},{3,4},{4,5},{5,6},{6,7},{7,8},{8,9},{9,10},{10,1... | collective-permute-start | bytes 21176 | tf_op jit(solution)/shard_map/ppermute | solution.py:36
  12.9 1.3 collective-permute-start.3
  14.4 1.4 collective-permute-done.2
  15.8 4.1 %collective-permute-done.3 = f32[2,98,9]{2,1,0:T(8,128)S(1)} collective-permute-done((f32[2,98,9]{2,1,0:T(8,128)S(1)}, f32[2,98,9]{2,1,0:T(8,128)S(1)}, u32[]{:S(2)}, u32[]{:S(2)}) %collective-permute-start.3) | collective-permute-done | bytes 7088 | tf_op jit(solution)/shard_map/ppermute | solution.py:39
  19.9 0.9 pad_maximum_fusion.1
  20.9 0.2 fusion.78
  21.3 0.1 slice.278
  21.4 0.1 slice.279
  21.7 0.1 subtract_divide_fusion
  21.8 3.2 %convert_multiply_fusion = f32[96,96,128]{2,1,0:T(8,128)S(1)} fusion(bf16[96,96,128]{2,1,0:T(8,128)(2,1)} %param.4, f32[96,96]{1,0:T(8,128)S(1)} %get-tuple-element.19), kind=kLoop, calls=%fused_computation.99 | loop fusion | flops 2359296 | bytes 7114752 | tf_op jit(solution)/shard_map/mul | solution.py:90
  25.1 15.2 %fusion.20 = f32[96,96,128]{2,1,0:T(8,128)S(1)} fusion(f32[96,96,128]{2,1,0:T(8,128)S(1)} %convert_multiply_fusion, f32[96,96]{1,0:T(8,128)S(1)} %slice.282, f32[96,96]{1,0:T(8,128)S(1)} %slice.281, f32[96,96]{1,0:T(8,128)S(1)} %slice.280, f32[96,96]{1,0:T(8,128)S(1)} %slice.279, f32[96,96]{1,0:T(8,128)S(1)} %slice.278, f32[96,96]{1,0:T(8,128)S(1)} %slice.277, ...), kind=kLoop, calls=%fused_computation.53 | loop fusion | flops 23592960 | bytes 9805824 | tf_op jit(solution)/shard_map/sub | solution.py:93
  40.3 15.2 %fusion.39 = f32[96,96,128]{2,1,0:T(8,128)S(1)} fusion(f32[96,96,128]{2,1,0:T(8,128)S(1)} %fusion.20, f32[96,96]{1,0:T(8,128)S(1)} %slice.282, f32[96,96]{1,0:T(8,128)S(1)} %slice.281, f32[96,96]{1,0:T(8,128)S(1)} %slice.280, f32[96,96]{1,0:T(8,128)S(1)} %slice.279, f32[96,96]{1,0:T(8,128)S(1)} %slice.278, f32[96,96]{1,0:T(8,128)S(1)} %slice.277, ...), kind=kLoop, calls=%fused_computation.72 | loop fusion | flops 23592960 | bytes 9805824 | tf_op jit(solution)/shard_map/sub | solution.py:93
  55.4 15.2 %fusion.66 = bf16[96,96,128]{2,1,0:T(8,128)(2,1)S(1)} fusion(f32[96,96,128]{2,1,0:T(8,128)S(1)} %fusion.39, f32[96,96]{1,0:T(8,128)S(1)} %slice.282, f32[96,96]{1,0:T(8,128)S(1)} %slice.281, f32[96,96]{1,0:T(8,128)S(1)} %slice.280, f32[96,96]{1,0:T(8,128)S(1)} %slice.279, f32[96,96]{1,0:T(8,128)S(1)} %slice.278, f32[96,96]{1,0:T(8,128)S(1)} %slice.277, ...), kind=kLoop, calls=%fused_computation.100 | loop fusion | flops 24772608 | bytes 7446528 | tf_op jit(solution)/shard_map/convert_element_type | solution.py:94
  70.7 0.7 pad_convert_fusion
  71.4 13.6 %fusion.1 = bf16[98,98,128]{2,1,0:T(8,128)(2,1)S(1)} fusion(f32[100,100,128]{2,1,0:T(8,128)S(1)} %pad_convert_fusion, f32[98,98]{1,0:T(8,128)S(1)} %get-tuple-element.10, f32[98,98]{1,0:T(8,128)S(1)} %get-tuple-element.9, f32[98,98]{1,0:T(8,128)S(1)} %get-tuple-element.8, f32[98,98]{1,0:T(8,128)S(1)} %get-tuple-element.7, f32[98,98]{1,0:T(8,128)S(1)} %get-tuple-element.6, ...), kind=kLoop, calls=%fused_computation.2 | loop fusion | flops 22127616 | bytes 47059600 | tf_op jit(solution)/shard_map/convert_element_type | solution.py:98
  85.1 3.4 %collective-permute-start.10 = (bf16[17,17,128]{2,1,0:T(8,128)(2,1)S(1)}, bf16[17,17,128]{2,1,0:T(8,128)(2,1)S(1)}, u32[]{:S(2)}, u32[]{:S(2)}) collective-permute-start(bf16[17,17,128]{2,1,0:T(8,128)(2,1)S(1)} %get-tuple-element.11), channel_id=1, source_target_pairs={{0,1},{1,2},{2,3},{3,4},{4,5},{5,6},{6,7},{7,8},{8,9},{9,10},{10,1... | collective-permute-start | bytes 221960 | tf_op jit(solution)/shard_map/ppermute | solution.py:28
  88.5 1.3 collective-permute-start.4
  89.8 0.9 collective-permute-done.10
  90.7 1.9 collective-permute-start.11
  92.6 4.0 %collective-permute-done.4 = bf16[17,17,128]{2,1,0:T(8,128)(2,1)S(1)} collective-permute-done((bf16[17,17,128]{2,1,0:T(8,128)(2,1)S(1)}, bf16[17,17,128]{2,1,0:T(8,128)(2,1)S(1)}, u32[]{:S(2)}, u32[]{:S(2)}) %collective-permute-start.4) | collective-permute-done | bytes 74016 | tf_op jit(solution)/shard_map/ppermute | solution.py:28
  96.6 1.9 collective-permute-start.5
  98.5 0.9 fusion.74
  99.4 0.8 fusion.79
  100.2 1.3 collective-permute-start.12
  101.5 0.2 fusion.76
  101.8 9.6 %collective-permute-start.6 = (f32[128,128]{0,1:T(8,128)S(1)}, f32[128,128]{0,1:T(8,128)S(1)}, u32[]{:S(2)}, u32[]{:S(2)}) collective-permute-start(f32[128,128]{0,1:T(8,128)S(1)} %bitcast.66), channel_id=1, source_target_pairs={{0,1},{1,2},{2,3},{3,4},{4,5},{5,6},{6,7},{7,8},{8,9},{9,10},{10,1... | collective-permute-start | bytes 196616 | tf_op jit(solution)/shard_map/ppermute | solution.py:28
  111.4 0.9 fusion.69
  112.4 0.3 slice.298
  112.7 0.9 slice.295
  113.5 0.8 copy.26
  114.4 1.3 collective-permute-start.14
  115.7 3.1 %collective-permute-start.8 = (bf16[17,96,128]{2,1,0:T(8,128)(2,1)}, bf16[17,96,128]{2,1,0:T(8,128)(2,1)}, u32[]{:S(2)}, u32[]{:S(2)}) collective-permute-start(bf16[17,96,128]{2,1,0:T(8,128)(2,1)} %slice.295), channel_id=1, source_target_pairs={{16,0},{32,16},{48,32},{64,48},{80,64},{96,80},{112,96},{128,112},... | collective-permute-start | bytes 1253384 | tf_op jit(solution)/shard_map/ppermute | solution.py:28
  118.8 1.9 collective-permute-start.13
  120.7 3.4 %collective-permute-start.7 = (f32[128,128]{0,1:T(8,128)S(1)}, f32[128,128]{0,1:T(8,128)S(1)}, u32[]{:S(2)}, u32[]{:S(2)}) collective-permute-start(f32[128,128]{0,1:T(8,128)S(1)} %collective-permute-done.6), channel_id=1, source_target_pairs={{0,16},{16,32},{32,48},{48,64},{64,80},{80,96},{96,112},{112,128},... | collective-permute-start | bytes 196616 | tf_op jit(solution)/shard_map/ppermute | solution.py:28
  124.1 0.2 fusion.82
  124.4 0.8 copy.22
  125.2 23.0 %all-to-all-start = ((f32[16,2,1024]{2,1,0:T(2,128)}), f32[16,2,1024]{2,1,0:T(2,128)}, u32[]{:S(2)}, u32[]{:S(2)}) async-start(f32[16,2,1024]{2,1,0:T(2,128)} %copy.22), calls=%async_computation | async-start | bytes 262144 | tf_op jit(solution)/shard_map/all_to_all | solution.py:214
  148.2 0.7 copy.25
  148.9 0.1 copy.23
  149.0 1.3 fusion.91
  150.3 1.9 collective-permute-start.9
  152.3 1.3 fusion.72
  153.6 3.8 %collective-permute-start.15 = (f32[128,128]{0,1:T(8,128)S(1)}, f32[128,128]{0,1:T(8,128)S(1)}, u32[]{:S(2)}, u32[]{:S(2)}) collective-permute-start(f32[128,128]{0,1:T(8,128)S(1)} %bitcast.67), channel_id=1, source_target_pairs={{0,1},{1,2},{2,3},{3,4},{4,5},{5,6},{6,7},{7,8},{8,9},{9,10},{10,1... | collective-permute-start | bytes 196616 | tf_op jit(solution)/shard_map/ppermute | solution.py:28
  157.4 0.1 copy.24
  157.5 0.8 bitcast_dynamic-update-slice_fusion.5
  158.3 0.9 collective-permute-done.15
  159.3 0.1 copy.28
  159.4 0.8 bitcast_dynamic-update-slice_fusion.2
  160.2 0.8 bitcast_dynamic-update-slice_fusion
  161.1 0.1 reshape.137
  161.2 0.6 fusion.80
  161.9 1.8 copy.30
  163.7 1.3 all-to-all-done
  165.0 20.2 %all-to-all-start.1 = ((f32[16,2,8192]{2,1,0:T(2,128)}), f32[16,2,8192]{2,1,0:T(2,128)S(1)}, u32[]{:S(2)}, u32[]{:S(2)}) async-start(f32[16,2,8192]{2,1,0:T(2,128)} %copy.30), calls=%async_computation.1 | async-start | bytes 2097152 | tf_op jit(solution)/shard_map/all_to_all | solution.py:215
  185.2 1.7 reshape.128
  186.9 25.5 %all-to-all-done.1 = f32[16,2,8192]{2,1,0:T(2,128)S(1)} async-done(((f32[16,2,8192]{2,1,0:T(2,128)}), f32[16,2,8192]{2,1,0:T(2,128)S(1)}, u32[]{:S(2)}, u32[]{:S(2)}) %all-to-all-start.1) | async-done | bytes 1048608 | tf_op jit(solution)/shard_map/all_to_all | solution.py:215
  212.4 1.9 reshape.130
  (39 shorter events, 0.9 us)
Async XLA Ops:
  1.4 7.2 %collective-permute-start = (f32[2,9,80]{2,1,0:T(8,128)S(1)}, f32[2,9,80]{2,1,0:T(8,128)S(1)}, u32[]{:S(2)}, u32[]{:S(2)}) collective-permute-start(f32[2,9,80]{2,1,0:T(8,128)S(1)} %get-tuple-element.15), channel_id=1, source_target_pairs={{0,16},{16,32},{32,48},{48,64},{64,80},{80,96},{96,112},{112,128},... | collective-permute-start | bytes 17288 | tf_op jit(solution)/shard_map/ppermute | solution.py:36
  3.3 5.3 %collective-permute-start.1 = (f32[2,9,80]{2,1,0:T(8,128)S(1)}, f32[2,9,80]{2,1,0:T(8,128)S(1)}, u32[]{:S(2)}, u32[]{:S(2)}) collective-permute-start(f32[2,9,80]{2,1,0:T(8,128)S(1)} %get-tuple-element.16), channel_id=1, source_target_pairs={{16,0},{32,16},{48,32},{64,48},{80,64},{96,80},{112,96},{128,112},... | collective-permute-start | bytes 17288 | tf_op jit(solution)/shard_map/ppermute | solution.py:39
  9.5 6.3 %collective-permute-start.2 = (f32[2,98,9]{2,1,0:T(8,128)S(1)}, f32[2,98,9]{2,1,0:T(8,128)S(1)}, u32[]{:S(2)}, u32[]{:S(2)}) collective-permute-start(f32[2,98,9]{2,1,0:T(8,128)S(1)} %get-tuple-element.13), channel_id=1, source_target_pairs={{0,1},{1,2},{2,3},{3,4},{4,5},{5,6},{6,7},{7,8},{8,9},{9,10},{10,1... | collective-permute-start | bytes 21176 | tf_op jit(solution)/shard_map/ppermute | solution.py:36
  12.9 7.0 %collective-permute-start.3 = (f32[2,98,9]{2,1,0:T(8,128)S(1)}, f32[2,98,9]{2,1,0:T(8,128)S(1)}, u32[]{:S(2)}, u32[]{:S(2)}) collective-permute-start(f32[2,98,9]{2,1,0:T(8,128)S(1)} %get-tuple-element.14), channel_id=1, source_target_pairs={{1,0},{2,1},{3,2},{4,3},{5,4},{6,5},{7,6},{8,7},{9,8},{10,9},{11,1... | collective-permute-start | bytes 21176 | tf_op jit(solution)/shard_map/ppermute | solution.py:39
  71.4 17.1 %copy-start.1 = (s32[1,1,16,1]{2,3,1,0:T(1,128)S(1)}, s32[1,1,16,1]{2,3,1,0:T(1,128)}, u32[]{:S(2)}) copy-start(s32[1,1,16,1]{2,3,1,0:T(1,128)} %param.7) | copy-start | bytes 196
  85.1 5.7 %collective-permute-start.10 = (bf16[17,17,128]{2,1,0:T(8,128)(2,1)S(1)}, bf16[17,17,128]{2,1,0:T(8,128)(2,1)S(1)}, u32[]{:S(2)}, u32[]{:S(2)}) collective-permute-start(bf16[17,17,128]{2,1,0:T(8,128)(2,1)S(1)} %get-tuple-element.11), channel_id=1, source_target_pairs={{0,1},{1,2},{2,3},{3,4},{4,5},{5,6},{6,7},{7,8},{8,9},{9,10},{10,1... | collective-permute-start | bytes 221960 | tf_op jit(solution)/shard_map/ppermute | solution.py:28
  88.5 8.1 %collective-permute-start.4 = (bf16[17,17,128]{2,1,0:T(8,128)(2,1)S(1)}, bf16[17,17,128]{2,1,0:T(8,128)(2,1)S(1)}, u32[]{:S(2)}, u32[]{:S(2)}) collective-permute-start(bf16[17,17,128]{2,1,0:T(8,128)(2,1)S(1)} %get-tuple-element.12), channel_id=1, source_target_pairs={{1,0},{2,1},{3,2},{4,3},{5,4},{6,5},{7,6},{8,7},{9,8},{10,9},{11,1... | collective-permute-start | bytes 221960 | tf_op jit(solution)/shard_map/ppermute | solution.py:28
  90.7 7.8 %collective-permute-start.11 = (bf16[17,17,128]{2,1,0:T(8,128)(2,1)S(1)}, bf16[17,17,128]{2,1,0:T(8,128)(2,1)S(1)}, u32[]{:S(2)}, u32[]{:S(2)}) collective-permute-start(bf16[17,17,128]{2,1,0:T(8,128)(2,1)S(1)} %collective-permute-done.10), channel_id=1, source_target_pairs={{16,0},{32,16},{48,32},{64,48},{80,64},{96,80},{112,96},{128,112},... | collective-permute-start | bytes 221960 | tf_op jit(solution)/shard_map/ppermute | solution.py:28
  96.6 4.9 %collective-permute-start.5 = (bf16[17,17,128]{2,1,0:T(8,128)(2,1)S(1)}, bf16[17,17,128]{2,1,0:T(8,128)(2,1)S(1)}, u32[]{:S(2)}, u32[]{:S(2)}) collective-permute-start(bf16[17,17,128]{2,1,0:T(8,128)(2,1)S(1)} %collective-permute-done.4), channel_id=1, source_target_pairs={{16,0},{32,16},{48,32},{64,48},{80,64},{96,80},{112,96},{128,112},... | collective-permute-start | bytes 221960 | tf_op jit(solution)/shard_map/ppermute | solution.py:28
  100.2 18.5 %collective-permute-start.12 = (bf16[128,128]{0,1:T(8,128)(2,1)S(1)}, bf16[128,128]{0,1:T(8,128)(2,1)S(1)}, u32[]{:S(2)}, u32[]{:S(2)}) collective-permute-start(bf16[128,128]{0,1:T(8,128)(2,1)S(1)} %fusion.79), channel_id=1, source_target_pairs={{1,0},{2,1},{3,2},{4,3},{5,4},{6,5},{7,6},{8,7},{9,8},{10,9},{11,1... | collective-permute-start | bytes 98312 | tf_op jit(solution)/shard_map/ppermute | solution.py:28
  101.8 19.0 %copy-start = (f32[128,128,1]{1,0,2:T(8,128)}, f32[128,128,1]{1,0,2:T(8,128)S(1)}, u32[]{:S(2)}) copy-start(f32[128,128,1]{1,0,2:T(8,128)S(1)} %fusion.76) | copy-start | bytes 196612
  101.8 18.9 %collective-permute-start.6 = (f32[128,128]{0,1:T(8,128)S(1)}, f32[128,128]{0,1:T(8,128)S(1)}, u32[]{:S(2)}, u32[]{:S(2)}) collective-permute-start(f32[128,128]{0,1:T(8,128)S(1)} %bitcast.66), channel_id=1, source_target_pairs={{0,1},{1,2},{2,3},{3,4},{4,5},{5,6},{6,7},{7,8},{8,9},{9,10},{10,1... | collective-permute-start | bytes 196616 | tf_op jit(solution)/shard_map/ppermute | solution.py:28
  114.4 37.9 %collective-permute-start.14 = (bf16[96,17,128]{2,0,1:T(8,128)(2,1)}, bf16[96,17,128]{2,0,1:T(8,128)(2,1)}, u32[]{:S(2)}, u32[]{:S(2)}) collective-permute-start(bf16[96,17,128]{2,0,1:T(8,128)(2,1)} %copy.26), channel_id=1, source_target_pairs={{1,0},{2,1},{3,2},{4,3},{5,4},{6,5},{7,6},{8,7},{9,8},{10,9},{11,1... | collective-permute-start | bytes 1253384 | tf_op jit(solution)/shard_map/ppermute | solution.py:28
  115.7 33.3 %collective-permute-start.8 = (bf16[17,96,128]{2,1,0:T(8,128)(2,1)}, bf16[17,96,128]{2,1,0:T(8,128)(2,1)}, u32[]{:S(2)}, u32[]{:S(2)}) collective-permute-start(bf16[17,96,128]{2,1,0:T(8,128)(2,1)} %slice.295), channel_id=1, source_target_pairs={{16,0},{32,16},{48,32},{64,48},{80,64},{96,80},{112,96},{128,112},... | collective-permute-start | bytes 1253384 | tf_op jit(solution)/shard_map/ppermute | solution.py:28
  118.8 29.4 %collective-permute-start.13 = (f32[128,128]{0,1:T(8,128)S(1)}, f32[128,128]{0,1:T(8,128)S(1)}, u32[]{:S(2)}, u32[]{:S(2)}) collective-permute-start(f32[128,128]{0,1:T(8,128)S(1)} %convert_element_type.53), channel_id=1, source_target_pairs={{0,16},{16,32},{32,48},{48,64},{64,80},{80,96},{96,112},{112,128},... | collective-permute-start | bytes 196616 | tf_op jit(solution)/shard_map/ppermute | solution.py:28
  120.7 28.1 %collective-permute-start.7 = (f32[128,128]{0,1:T(8,128)S(1)}, f32[128,128]{0,1:T(8,128)S(1)}, u32[]{:S(2)}, u32[]{:S(2)}) collective-permute-start(f32[128,128]{0,1:T(8,128)S(1)} %collective-permute-done.6), channel_id=1, source_target_pairs={{0,16},{16,32},{32,48},{48,64},{64,80},{80,96},{96,112},{112,128},... | collective-permute-start | bytes 196616 | tf_op jit(solution)/shard_map/ppermute | solution.py:28
  125.2 39.8 %all-to-all-start = ((f32[16,2,1024]{2,1,0:T(2,128)}), f32[16,2,1024]{2,1,0:T(2,128)}, u32[]{:S(2)}, u32[]{:S(2)}) async-start(f32[16,2,1024]{2,1,0:T(2,128)} %copy.22), calls=%async_computation | async-start | bytes 262144 | tf_op jit(solution)/shard_map/all_to_all | solution.py:214
  150.3 7.1 %collective-permute-start.9 = (f32[128,128]{0,1:T(8,128)S(1)}, f32[128,128]{0,1:T(8,128)S(1)}, u32[]{:S(2)}, u32[]{:S(2)}) collective-permute-start(f32[128,128]{0,1:T(8,128)S(1)} %bitcast.65), channel_id=1, source_target_pairs={{0,16},{16,32},{32,48},{48,64},{64,80},{80,96},{96,112},{112,128},... | collective-permute-start | bytes 196616 | tf_op jit(solution)/shard_map/ppermute | solution.py:28
  153.6 5.7 %collective-permute-start.15 = (f32[128,128]{0,1:T(8,128)S(1)}, f32[128,128]{0,1:T(8,128)S(1)}, u32[]{:S(2)}, u32[]{:S(2)}) collective-permute-start(f32[128,128]{0,1:T(8,128)S(1)} %bitcast.67), channel_id=1, source_target_pairs={{0,1},{1,2},{2,3},{3,4},{4,5},{5,6},{6,7},{7,8},{8,9},{9,10},{10,1... | collective-permute-start | bytes 196616 | tf_op jit(solution)/shard_map/ppermute | solution.py:28
  165.0 47.4 %all-to-all-start.1 = ((f32[16,2,8192]{2,1,0:T(2,128)}), f32[16,2,8192]{2,1,0:T(2,128)S(1)}, u32[]{:S(2)}, u32[]{:S(2)}) async-start(f32[16,2,8192]{2,1,0:T(2,128)} %copy.30), calls=%async_computation.1 | async-start | bytes 2097152 | tf_op jit(solution)/shard_map/all_to_all | solution.py:215
where the time goes:
time: 216 us; the launch traced here: 214 us
  starting transfers between devices  88.2 us (41%)
  other arithmetic  68.4 us (32%)
  waiting for transfers between devices  38.3 us (18%)
  local copies, waits for them, and re-layouts  12.7 us (6%)
  matrix products  5.52 us (3%)
    ppermute x12, starting transfers between devices, passed_along(): return lax.ppermute(block, axis, route)  34.8 us
    sub x2, other arithmetic, smooth_and_apply(): current = current - omega * (inverse[:, :, None] * applied)  30.4 us
    all_to_all x1, waiting for transfers between devices, on_device(): lax.all_to_all(send_cross, 'col', split_axis=0, concat_axis=0, tiled=True)  25.5 us
    all_to_all x1, starting transfers between devices, on_device(): lax.all_to_all(send_self, 'col', split_axis=0, concat_axis=0, tiled=True)  23 us
    all_to_all x1, starting transfers between devices, on_device(): lax.all_to_all(send_cross, 'col', split_axis=0, concat_axis=0, tiled=True)  20.2 us
    convert_element_type x1, other arithmetic, smooth_and_apply(): smoothed = lax.optimization_barrier(current.astype(jnp.bfloat16))  15.2 us
    convert_element_type x1, other arithmetic, smooth_and_apply(): return (smoothed, image.astype(jnp.bfloat16))  13.6 us
    ppermute x12, waiting for transfers between devices, passed_along(): return lax.ppermute(block, axis, route)  5.83 us
  transfers between devices with their start and end apart: 18, of which 7 were waited for; matrix products, arithmetic and copies ran while one was open for 8% of the time, Pallas kernels for 0%

commit v1 on v0

v1 whole, which is shorter than its diff:
```python
import functools
import math

import jax
import jax.numpy as jnp
from jax import lax
from jax.experimental import pallas as pl
from jax.experimental.pallas import tpu as pltpu
from jax.sharding import PartitionSpec as P

CELLS = 80
EXT = 96
MODES = 128
SWEEPS = 3
GROUPS = 16
FRAME = 112
CHUNK = 32
MESH = pl.DeviceIdType.MESH
F32 = jnp.float32
BF16 = jnp.bfloat16
PAIRS = ((1, 0), (0, 1), (1, 1), (1, -1))
VMEM = pl.BlockSpec(memory_space=pltpu.VMEM)
SMEM = pl.BlockSpec(memory_space=pltpu.SMEM)


def neighbour(da, db):
    rows, cols = lax.axis_size("row"), lax.axis_size("col")
    r, c = lax.axis_index("row"), lax.axis_index("col")
    return (lax.rem(r + da + rows, rows), lax.rem(c + db + cols, cols))


AROUND = tuple((a, b) for a in (-1, 0, 1) for b in (-1, 0, 1) if (a, b) != (0, 0))


def greet(others):
    barrier = pltpu.get_barrier_semaphore()
    for device in others:
        pl.semaphore_signal(barrier, inc=1, device_id=device, device_id_type=MESH)
    pl.semaphore_wait(barrier, len(others))


def lanes(shape):
    return lax.broadcasted_iota(jnp.int32, shape, 1)


def halo_kernel(k_ref, s_ref, out_ref, mid, side, left, right, send, recv):
    rows, cols = lax.axis_size("row"), lax.axis_size("col")
    r, c = lax.axis_index("row"), lax.axis_index("col")
    own = []
    for ref in (k_ref, s_ref):
        own.append(
            jnp.concatenate(
                [jnp.zeros((CELLS, 16), F32), ref[...], jnp.zeros((CELLS, 32), F32)], axis=1
            )
        )
    k, s = own
    lane = lanes((CELLS, 128))
    mid[0, 16:96, :] = k
    mid[1, 16:96, :] = s
    packed = jnp.where(lane < 64, pltpu.roll(s, 96, 1), 0.0)
    packed = jnp.where(lane < 48, pltpu.roll(k, 80, 1), packed)
    packed = jnp.where(lane < 32, s, packed)
    packed = jnp.where(lane < 16, pltpu.roll(k, 112, 1), packed)
    side[...] = packed
    greet([neighbour(a, b) for a, b in AROUND])
    plan = [
        ((-1, 0), mid.at[:, 16:32, :], mid.at[:, 96:112, :]),
        ((1, 0), mid.at[:, 80:96, :], mid.at[:, 0:16, :]),
        ((0, -1), side, right.at[16:96, :]),
        ((0, 1), side, left.at[16:96, :]),
        ((-1, -1), side.at[0:16, :], right.at[96:112, :]),
        ((-1, 1), side.at[0:16, :], left.at[96:112, :]),
        ((1, -1), side.at[64:80, :], right.at[0:16, :]),
        ((1, 1), side.at[64:80, :], left.at[0:16, :]),
    ]
    copies = []
    for n, ((a, b), src, dst) in enumerate(plan):
        copy = pltpu.make_async_remote_copy(
            src_ref=src,
            dst_ref=dst,
            send_sem=send.at[n],
            recv_sem=recv.at[n],
            device_id=neighbour(a, b),
            device_id_type=MESH,
        )
        copy.start()
        copies.append(copy)
    for copy in copies:
        copy.wait()
    lane = lanes((FRAME, 128))
    line = lax.broadcasted_iota(jnp.int32, (FRAME, 128), 0)
    first_a, last_a = jnp.where(r == 0, 16, 0), jnp.where(r == rows - 1, 96, FRAME)
    first_b, last_b = jnp.where(c == 0, 16, 0), jnp.where(c == cols - 1, 96, FRAME)
    inside = (line >= first_a) & (line < last_a) & (lane >= first_b) & (lane < last_b)
    low, high = left[...], right[...]
    for n, (shift_low, shift_high) in enumerate(((96, 96), (80, 80))):
        whole = jnp.where(lane < 96, mid[n], pltpu.roll(high, shift_high, 1))
        whole = jnp.where(lane < 16, pltpu.roll(low, shift_low, 1), whole)
        out_ref[n] = jnp.where(inside, whole, 0.0)
    out_ref[2] = inside.astype(F32)


def around(conductivity, storage):
    return pl.pallas_call(
        halo_kernel,
        out_shape=jax.ShapeDtypeStruct((3, FRAME, 128), F32),
        in_specs=[VMEM, VMEM],
        out_specs=VMEM,
        scratch_shapes=[
            pltpu.VMEM((2, FRAME, 128), F32),
            pltpu.VMEM((CELLS, 128), F32),
            pltpu.VMEM((FRAME, 128), F32),
            pltpu.VMEM((FRAME, 128), F32),
            pltpu.SemaphoreType.DMA((8,)),
            pltpu.SemaphoreType.DMA((8,)),
        ],
        compiler_params=pltpu.CompilerParams(collective_id=0, has_side_effects=True),
    )(conductivity, storage)


def omegas():
    return [
        1.0 / (1.15 + 0.85 * math.cos(math.pi * (2 * t + 1) / (2 * SWEEPS))) for t in range(SWEEPS)
    ]


def across(ref, line, start):
    low = ref[line, pl.ds(start - 1, CHUNK), :]
    mid = ref[line, pl.ds(pl.multiple_of(start, 8), CHUNK), :]
    high = ref[line, pl.ds(start + 1, CHUNK), :]
    return mid, (low + high) + (mid + mid)


def walk(z_ref, q_ref, first, last, unroll, body):
    @pl.loop(0, EXT // CHUNK)
    def _(chunk):
        start = 8 + chunk * CHUNK
        zc, hz = across(z_ref, first, start)
        qc, hq = across(q_ref, first, start)
        _, hz0 = across(z_ref, first - 1, start)
        _, hq0 = across(q_ref, first - 1, start)

        def step(line, carry):
            zc, hz, pz, qc, hq, pq = carry
            zn, hzn = across(z_ref, line + 1, start)
            qn, hqn = across(q_ref, line + 1, start)
            pzn, pqn = hz + hzn, hq + hqn
            body(line, start, zc, qc, pz + pzn, pq + pqn)
            return zn, hzn, pzn, qn, hqn, pqn

        lax.fori_loop(
            first, last, step, (zc, hz, hz0 + hz, qc, hq, hq0 + hq), unroll=unroll
        )


def smooth_kernel(
    coef_ref, modes_ref, owners_ref,
    row_s, row_i, col_s, col_i, edges, corners, self_ref, place_ref,
    kb, gb, db, za, qa, zb, qb, s_all, i_all,
):
    k, s, inside = coef_ref[0], coef_ref[1], coef_ref[2]
    kp = jnp.concatenate([k, jnp.zeros((128 - FRAME, 128), F32)], axis=0)

    def three(x, axis):
        return pltpu.roll(x, 1, axis) + pltpu.roll(x, 127, axis) + 2.0 * x

    total = three(three(kp, 0), 1)[:FRAME]
    diagonal = s + 2.0 * k + 0.25 * total
    inverse = inside / (diagonal + (1.0 - inside))
    columns = []
    for x in (k, inverse, diagonal):
        xp = jnp.concatenate([x, jnp.zeros((128 - FRAME, 128), F32)], axis=0)
        columns.append(xp.T[8 : 8 + EXT])
    omega = omegas()
    scale = 1.0
    for w in omega:
        scale = scale * w / 4.0
    edge = jnp.zeros((8, MODES), F32)
    for ref in (za, qa, zb, qb):
        for line in (0, 1, EXT + 2, EXT + 3):
            ref[line] = jnp.zeros((FRAME, MODES), F32)
    for line in range(2, EXT + 2):
        for ref in (za, qa, zb, qb):
            ref[line, 0:8, :] = edge
            ref[line, 104:112, :] = edge
    for line in range(1, EXT + 3):
        at = line + 6
        kx = jnp.broadcast_to(columns[0][:, at : at + 1], (EXT, MODES))
        kb[line] = kx
        if 2 <= line < EXT + 2:
            gx = jnp.broadcast_to(columns[1][:, at : at + 1], (EXT, MODES))
            gb[line] = gx
            db[line] = jnp.broadcast_to(columns[2][:, at : at + 1], (EXT, MODES))
            z = jnp.where(gx > 0.0, modes_ref[line - 2].astype(F32) * scale, 0.0)
            za[line, 8:104, :] = z
            qa[line, 8:104, :] = kx * z
        else:
            db[line] = jnp.zeros((EXT, MODES), F32)

    def inner(ref, line, start):
        return ref[line, pl.ds(pl.multiple_of(start - 8, 8), CHUNK), :]

    buffers = ((za, qa), (zb, qb))
    for t in range(SWEEPS):
        (z_ref, q_ref), (z_to, q_to) = buffers[t % 2], buffers[(t + 1) % 2]
        ratio = (1.0 - omega[t]) * 4.0 / omega[t]

        def sweep(line, start, z, q, u, v, t=t, z_to=z_to, q_to=q_to, ratio=ratio):
            kx = inner(kb, line, start)
            new = ratio * z + inner(gb, line, start) * (kx * u + (v - 8.0 * q))
            here = pl.ds(pl.multiple_of(start, 8), CHUNK)
            if t == SWEEPS - 1:
                rounded = new.astype(BF16)
                s_all[line - 2, pl.ds(pl.multiple_of(start - 8, 16), CHUNK), :] = rounded
                new = rounded.astype(F32)
            z_to[line, here, :] = new
            q_to[line, here, :] = kx * new

        walk(z_ref, q_ref, 2, EXT + 2, 2, sweep)

    z_ref, q_ref = buffers[SWEEPS % 2]

    def image(line, start, z, q, u, v):
        value = inner(db, line, start) * z + 2.0 * q - 0.25 * (inner(kb, line, start) * u + v)
        i_all[line - 1, pl.ds(pl.multiple_of(start - 8, 16), CHUNK), :] = value.astype(BF16)

    walk(z_ref, q_ref, 1, EXT + 3, 2, image)

    total_self = jnp.zeros((MODES, MODES), F32)
    for a in range(0, EXT, 8):
        total_self += lax.dot_general(
            s_all[a : a + 8].reshape(8 * EXT, MODES),
            i_all[a + 1 : a + 9].reshape(8 * EXT, MODES),
            (((0,), (0,)), ((), ())),
            preferred_element_type=F32,
        )
    self_ref[...] = total_self.astype(BF16)

    row_s[...] = s_all[79:96]
    row_i[...] = i_all[0:17]
    col_s[:, 0:16, :] = s_all[:, 0:16, :]
    col_s[:, 16:32, :] = s_all[:, 80:96, :]
    col_i[:, 0:16, :] = i_all[0:98, 0:16, :]
    col_i[:, 16:32, :] = i_all[0:98, 80:96, :]

    def ring(column, lane):
        z, q = z_ref[:, column, :], q_ref[:, column, :]
        u = z[0:98] + z[2:100] + 2.0 * z[1:99]
        v = q[0:98] + q[2:100] + 2.0 * q[1:99]
        return -0.25 * (k[7:105, lane : lane + 1] * u + v)

    low, high = ring(8, 7), ring(103, 104)
    s_low, s_high = z_ref[2:98, 8 + 16, :], z_ref[2:98, 8 + 79, :]
    for n, part in enumerate((low[1:49], s_high[0:48], s_high[48:96], low[49:97])):
        edges[n] = part.astype(BF16)
    for n, part in enumerate(
        (low[0:9], s_high[79:88], s_high[88:96], low[9:17],
         high[0:9], s_low[79:88], s_low[88:96], high[9:17])
    ):
        filled = jnp.concatenate([part, jnp.zeros((16 - part.shape[0], MODES), F32)], axis=0)
        corners[n] = filled.astype(BF16)

    places = place_ref.shape[0]
    most = places // 8 // lax.axis_size("col")
    lane = lax.broadcasted_iota(jnp.int32, (places, MODES), 1)
    line = lax.broadcasted_iota(jnp.int32, (places, MODES), 0)
    slot = jnp.full((places, MODES), -1, jnp.int32)
    names = [owners_ref[0, g] for g in range(GROUPS)]
    for g in range(GROUPS):
        rank = jnp.int32(0)
        for earlier in range(g):
            rank = rank + (names[earlier] == names[g]).astype(jnp.int32)
        slot = jnp.where(lane // 8 == g, names[g] * most + rank, slot)
    found = (line // 8 == slot) & (line % 8 == lane % 8)
    place_ref[...] = found.astype(F32).astype(BF16)


def smooth(coefficients, modes, owners, places):
    shape = jax.ShapeDtypeStruct
    return pl.pallas_call(
        smooth_kernel,
        out_shape=(
            shape((17, EXT, MODES), BF16),
            shape((17, EXT, MODES), BF16),
            shape((EXT, 32, MODES), BF16),
            shape((EXT + 2, 32, MODES), BF16),
            shape((4, 48, MODES), BF16),
            shape((8, 16, MODES), BF16),
            shape((MODES, MODES), BF16),
            shape((places, MODES), BF16),
        ),
        in_specs=[VMEM, VMEM, SMEM],
        out_specs=(VMEM,) * 8,
        scratch_shapes=[pltpu.VMEM((EXT + 4, EXT, MODES), F32)] * 3
        + [pltpu.VMEM((EXT + 4, FRAME, MODES), F32)] * 4
        + [pltpu.VMEM((EXT, EXT, MODES), BF16), pltpu.VMEM((EXT + 2, EXT, MODES), BF16)],
        compiler_params=pltpu.CompilerParams(vmem_limit_bytes=60 * 2**20),
    )(coefficients, modes, owners)


def contract(first, second):
    return lax.dot_general(
        first.reshape(-1, MODES),
        second.reshape(-1, MODES),
        (((0,), (0,)), ((), ())),
        preferred_element_type=F32,
    )


def exchange_kernel(
    row_s, row_i, col_s, col_i, edges, corners, self_ref, place_ref, out_ref,
    row_2, row_1, col_2, col_1, cor_2, cor_1, edge_in, corner_in, partial_out, partial_in, outgoing,
    send, recv, psend, precv, asend, arecv,
):
    rows, cols = lax.axis_size("row"), lax.axis_size("col")
    r, c = lax.axis_index("row"), lax.axis_index("col")
    greet(
        [neighbour(a, b) for a, b in AROUND] + [neighbour(0, d) for d in range(1, cols)]
    )
    plan = []
    for n, (a, b) in enumerate(PAIRS):
        down, up = (-a, -b), (a, b)
        if n == 0:
            plan.append((down, row_i.at[0:9], row_2))
            plan.append((up, row_s.at[9:17], row_1))
        elif n == 1:
            plan.append((down, col_i.at[1:49, 0:16], col_2))
            plan.append((down, edges.at[0], edge_in.at[0]))
            plan.append((up, col_s.at[48:96, 16:32], col_1))
            plan.append((up, edges.at[2], edge_in.at[1]))
        else:
            m = n - 2
            image_cols = pl.ds(16 * m, 16)
            mode_cols = pl.ds(16 - 16 * m, 16)
            plan.append((down, col_i.at[0:9, image_cols], cor_2.at[m]))
            plan.append((down, corners.at[4 * m], corner_in.at[2 * m]))
            plan.append((up, col_s.at[88:96, mode_cols], cor_1.at[m]))
            plan.append((up, corners.at[4 * m + 2], corner_in.at[2 * m + 1]))
    copies = []
    for n, (to, src, dst) in enumerate(plan):
        copy = pltpu.make_async_remote_copy(
            src_ref=src,
            dst_ref=dst,
            send_sem=send.at[n],
            recv_sem=recv.at[n],
            device_id=neighbour(*to),
            device_id_type=MESH,
        )
        copy.start()
        copies.append(copy)

    place = place_ref[...]

    def put(slot, block, transposed):
        dims = (((1,), (1 if transposed else 0,)), ((), ()))
        rows_out = lax.dot_general(place, block, dims, preferred_element_type=F32)
        outgoing[:, slot] = rows_out.astype(BF16).reshape(cols, -1, MODES)

    put(0, self_ref[...], False)

    halves = []
    order = (2, 3, 0, 1)
    first_of = {0: 0, 1: 2, 2: 6, 3: 10}
    halves = {}
    pcopies = {}
    for n in order:
        base = first_of[n]
        a, b = PAIRS[n]
        if n == 0:
            copies[base].wait_recv()
            lower = contract(row_s[0:9], row_2[...])
            copies[base + 1].wait_recv()
            upper = contract(row_1[...], row_i[9:17])
        elif n == 1:
            copies[base].wait_recv()
            copies[base + 1].wait_recv()
            lower = contract(col_s[0:48, 16:32], col_2[...]) + contract(edges[1], edge_in[0])
            copies[base + 2].wait_recv()
            copies[base + 3].wait_recv()
            upper = contract(col_1[...], col_i[49:97, 0:16]) + contract(edge_in[1], edges[3])
        else:
            m = n - 2
            image_cols = slice(16 * m, 16 * m + 16)
            mode_cols = slice(16 - 16 * m, 32 - 16 * m)
            copies[base].wait_recv()
            copies[base + 1].wait_recv()
            lower = contract(col_s[79:88, mode_cols], cor_2[m]) + contract(
                corners[4 * m + 1], corner_in[2 * m]
            )
            copies[base + 2].wait_recv()
            copies[base + 3].wait_recv()
            upper = contract(cor_1[m], col_i[9:17, image_cols]) + contract(
                corner_in[2 * m + 1], corners[4 * m + 3]
            )
        partial_out[2 * n] = lower.astype(BF16)
        partial_out[2 * n + 1] = upper.astype(BF16)
        halves[n] = (lower, upper)
        for half, to in ((0, (a, b)), (1, (-a, -b))):
            copy = pltpu.make_async_remote_copy(
                src_ref=partial_out.at[2 * n + half],
                dst_ref=partial_in.at[2 * n + half],
                send_sem=psend.at[2 * n + half],
                recv_sem=precv.at[2 * n + half],
                device_id=neighbour(*to),
                device_id_type=MESH,
            )
            copy.start()
            pcopies[2 * n + half] = copy
    as_lower = {0: 7, 1: 5, 2: 8, 3: 6}
    as_upper = {0: 2, 1: 4, 2: 1, 3: 3}
    for n in order:
        a, b = PAIRS[n]
        lower, upper = halves[n]
        pcopies[2 * n + 1].wait_recv()
        valid = (r + a < rows) & (c + b >= 0) & (c + b < cols)
        block = lower + partial_in[2 * n + 1].astype(F32)
        put(as_lower[n], jnp.where(valid, block, 0.0).astype(BF16), False)
        pcopies[2 * n].wait_recv()
        valid = (r - a >= 0) & (c - b >= 0) & (c - b < cols)
        block = upper + partial_in[2 * n].astype(F32)
        put(as_upper[n], jnp.where(valid, block, 0.0).astype(BF16), True)
    for copy in copies:
        copy.wait_send()
    for copy in pcopies.values():
        copy.wait_send()

    out_ref[c] = outgoing[c]
    acopies = []
    for d in range(1, cols):
        to = neighbour(0, d)
        copy = pltpu.make_async_remote_copy(
            src_ref=outgoing.at[to[1]],
            dst_ref=out_ref.at[c],
            send_sem=asend.at[d],
            recv_sem=arecv.at[d],
            device_id=to,
            device_id_type=MESH,
        )
        copy.start()
        acopies.append(copy)
    for copy in acopies:
        copy.wait()


def exchange(parts, cols, places):
    per = places // cols
    shape = (cols, 9, per, MODES)
    dma = pltpu.SemaphoreType.DMA
    return pl.pallas_call(
        exchange_kernel,
        out_shape=jax.ShapeDtypeStruct(shape, BF16),
        in_specs=[VMEM] * 8,
        out_specs=VMEM,
        scratch_shapes=[
            pltpu.VMEM((9, EXT, MODES), BF16),
            pltpu.VMEM((8, EXT, MODES), BF16),
            pltpu.VMEM((48, 16, MODES), BF16),
            pltpu.VMEM((48, 16, MODES), BF16),
            pltpu.VMEM((2, 9, 16, MODES), BF16),
            pltpu.VMEM((2, 8, 16, MODES), BF16),
            pltpu.VMEM((2, 48, MODES), BF16),
            pltpu.VMEM((4, 16, MODES), BF16),
            pltpu.VMEM((8, MODES, MODES), BF16),
            pltpu.VMEM((8, MODES, MODES), BF16),
            pltpu.VMEM(shape, BF16),
            dma((14,)),
            dma((14,)),
            dma((8,)),
            dma((8,)),
            dma((cols,)),
            dma((cols,)),
        ],
        compiler_params=pltpu.CompilerParams(
            collective_id=1, has_side_effects=True, vmem_limit_bytes=40 * 2**20
        ),
    )(*parts)


def spread_kernel(got_ref, self_ref, cross_ref):
    most = got_ref.shape[2] // 8
    for source in range(got_ref.shape[0]):
        for rank in range(most):
            rows = slice(8 * rank, 8 * rank + 8)
            self_ref[0, source * most + rank] = got_ref[source, 0].astype(F32)[rows]
            for s in range(8):
                cross_ref[0, source * most + rank, s] = got_ref[source, 1 + s].astype(F32)[rows]


def spread(got, slots):
    return pl.pallas_call(
        spread_kernel,
        out_shape=(
            jax.ShapeDtypeStruct((1, slots, 8, MODES), F32),
            jax.ShapeDtypeStruct((1, slots, 8, 8, MODES), F32),
        ),
        in_specs=[VMEM],
        out_specs=(VMEM, VMEM),
    )(got)


def on_device(modes, conductivity, storage, owners, slots, cols):
    places = slots * 8
    coefficients = around(conductivity, storage)
    parts = smooth(coefficients, modes, owners.reshape(1, GROUPS), places)
    got = exchange(parts, cols, places)
    return spread(got, slots)


def solution(mesh):
    cols = mesh.shape["col"]
    return jax.shard_map(
        functools.partial(on_device, slots=2 * cols, cols=cols),
        mesh=mesh,
        in_specs=(
            P("row", "col", None),
            P("row", "col"),
            P("row", "col"),
            P("row", "col", None, None),
        ),
        out_specs=(P("row", "col", None, None), P("row", "col", None, None, None)),
        check_vma=False,
    )
```

time: 216 us -> 109 us (0.50)
  the two profiles are of different devices: /device:TPU:96 before, /device:TPU:7 now
where the time goes in v1:
time: 109 us
  Pallas kernels  99.9 us (92%)
  local copies, waits for them, and re-layouts  8.24 us (8%)
    pallas_call x1, Pallas kernels, exchange(): pl.pallas_call(exchange_kernel, out_shape=jax.ShapeDtypeStruct(shape, BF1...  56.9 us
    pallas_call x1, Pallas kernels, smooth(): pl.pallas_call(smooth_kernel, out_shape=(shape((17, EXT, MODES), BF16), s...  26.1 us
    pallas_call x1, Pallas kernels, around(): pl.pallas_call(halo_kernel, out_shape=jax.ShapeDtypeStruct((3, FRAME, 128...  14.7 us
    unnamed x18, local copies, waits for them, and re-layouts  8.24 us

profile of v1, /device:TPU:7, one launch (start us, length us, event | category | flops | bytes accessed | tf_op | source)
XLA Modules:
  0.0 108.8 jit_solution(5377157251817225712)
XLA Ops:
  0.6 14.7 %shard_map.59.coef_ref = f32[3,112,128]{2,1,0:T(8,128)} custom-call(f32[80,80]{1,0:T(8,128)} %k_ref.1, f32[80,80]{1,0:T(8,128)} %s_ref.1), custom_call_target="tpu_custom_call" | custom-call | tf_op jit(solution)/shard_map/pallas_call | solution.py:104
  15.3 26.1 %shard_map.60 = (bf16[17,96,128]{2,1,0:T(8,128)(2,1)}, bf16[17,96,128]{2,1,0:T(8,128)(2,1)}, bf16[96,32,128]{2,1,0:T(8,128)(2,1)}, bf16[98,32,128]{2,1,0:T(8,128...) custom-call(f32[3,112,128]{2,1,0:T(8,128)} %shard_map.59.coef_ref, ...), custom_call_target="tpu_custom_call" | custom-call | tf_op jit(solution)/shard_map/pallas_call | solution.py:280
  41.4 0.0 copy-start.1
  41.4 1.1 %copy-done.1 = bf16[98,32,128]{2,1,0:T(8,128)(2,1)S(1)} copy-done((bf16[98,32,128]{2,1,0:T(8,128)(2,1)S(1)}, bf16[98,32,128]{2,1,0:T(8,128)(2,1)}, u32[]{:S(2)}) %copy-start.1) | copy-done | bytes 802840
  42.6 0.0 copy-start.2
  42.6 1.1 %copy-done.2 = bf16[96,32,128]{2,1,0:T(8,128)(2,1)S(1)} copy-done((bf16[96,32,128]{2,1,0:T(8,128)(2,1)S(1)}, bf16[96,32,128]{2,1,0:T(8,128)(2,1)}, u32[]{:S(2)}) %copy-start.2) | copy-done | bytes 786456
  43.7 0.0 copy-start.3
  43.7 1.0 copy-done.3
  44.7 0.0 copy-start.4
  44.7 1.0 copy-done.4
  45.7 0.0 copy-start.5
  45.7 0.8 copy-done.5
  46.6 0.0 copy-start.6
  46.6 0.8 copy-done.6
  47.4 0.0 copy-start.7
  47.4 0.8 copy-done.7
  48.1 0.0 copy-start.8
  48.1 0.8 copy-done.8
  48.9 56.9 %shard_map.61.got_ref = bf16[16,9,16,128]{3,2,1,0:T(8,128)(2,1)S(1)} custom-call(bf16[17,96,128]{2,1,0:T(8,128)(2,1)S(1)} %copy-done.3, bf16[17,96,128]{2,1,0:T(8,128)(2,1)S(1)} %copy-done.4, bf16[96,32,128]{2,1,0:T(8,128)(2,1)S(1)} %copy-done.2, bf16[98,32,128]{2,1,0:T(8,128)(2,1)S(1)} %copy-done.1, bf16[4,48,128]{2,1,0:T(8,128)(2,1)S(1)} %copy-done.6, ...), custom_call_target="tpu_custom_call" | custom-call | tf_op jit(solution)/shard_map/pallas_call | solution.py:449
  105.8 0.0 copy-start
  105.8 0.8 copy-done
  106.6 2.2 %shard_map.62 = (f32[1,32,8,128]{3,2,1,0:T(8,128)}, f32[1,32,8,8,128]{4,3,2,1,0:T(8,128)}) custom-call(bf16[16,9,16,128]{3,2,1,0:T(8,128)(2,1)} %copy-done), custom_call_target="tpu_custom_call" | custom-call | tf_op jit(solution)/shard_map/pallas_call | solution.py:490
Async XLA Ops:
  41.4 1.1 %copy-start.1 = (bf16[98,32,128]{2,1,0:T(8,128)(2,1)S(1)}, bf16[98,32,128]{2,1,0:T(8,128)(2,1)}, u32[]{:S(2)}) copy-start(bf16[98,32,128]{2,1,0:T(8,128)(2,1)} %get-tuple-element.13.col_i) | copy-start | bytes 2408452
  42.6 1.1 %copy-start.2 = (bf16[96,32,128]{2,1,0:T(8,128)(2,1)S(1)}, bf16[96,32,128]{2,1,0:T(8,128)(2,1)}, u32[]{:S(2)}) copy-start(bf16[96,32,128]{2,1,0:T(8,128)(2,1)} %get-tuple-element.12.col_s) | copy-start | bytes 2359300
  43.7 1.0 copy-start.3
  44.7 1.0 copy-start.4
  45.7 0.8 copy-start.5
  46.6 0.8 copy-start.6
  47.4 0.8 copy-start.7
  48.1 0.8 copy-start.8
  105.8 0.8 copy-start

commit v2 on v0

v2 whole, which is shorter than its diff:
```python
import functools
import math

import jax
import jax.numpy as jnp
from jax import lax
from jax.experimental import pallas as pl
from jax.experimental.pallas import tpu as pltpu
from jax.sharding import PartitionSpec as P

CELLS = 80
EXT = 96
MODES = 128
SWEEPS = 3
GROUPS = 16
FRAME = 112
CHUNK = 32
MESH = pl.DeviceIdType.MESH
F32 = jnp.float32
BF16 = jnp.bfloat16
VMEM = pl.BlockSpec(memory_space=pltpu.VMEM)
SMEM = pl.BlockSpec(memory_space=pltpu.SMEM)
BLOCKS = (22, 54, 86, 98)
UNROLL = 8


def neighbour(da, db):
    rows, cols = lax.axis_size("row"), lax.axis_size("col")
    r, c = lax.axis_index("row"), lax.axis_index("col")
    return (lax.rem(r + da + rows, rows), lax.rem(c + db + cols, cols))


AROUND = tuple((a, b) for a in (-1, 0, 1) for b in (-1, 0, 1) if (a, b) != (0, 0))


def omegas():
    return [
        1.0 / (1.15 + 0.85 * math.cos(math.pi * (2 * t + 1) / (2 * SWEEPS))) for t in range(SWEEPS)
    ]


def remote(src, dst, send, recv, to):
    return pltpu.make_async_remote_copy(
        src_ref=src, dst_ref=dst, send_sem=send, recv_sem=recv, device_id=to, device_id_type=MESH
    )


def lanes(shape):
    return lax.broadcasted_iota(jnp.int32, shape, 1)


def across(ref, line, start):
    low = ref[line, pl.ds(start - 1, CHUNK), :]
    mid = ref[line, pl.ds(pl.multiple_of(start, 8), CHUNK), :]
    high = ref[line, pl.ds(start + 1, CHUNK), :]
    return mid, (low + high) + (mid + mid)


def walk(z_ref, q_ref, first, last, body):
    @pl.loop(0, EXT // CHUNK)
    def _(chunk):
        start = 8 + chunk * CHUNK
        zc, hz = across(z_ref, first, start)
        qc, hq = across(q_ref, first, start)
        _, hz0 = across(z_ref, first - 1, start)
        _, hq0 = across(q_ref, first - 1, start)

        def step(line, carry):
            zc, hz, pz, qc, hq, pq = carry
            zn, hzn = across(z_ref, line + 1, start)
            qn, hqn = across(q_ref, line + 1, start)
            pzn, pqn = hz + hzn, hq + hqn
            body(line, start, zc, qc, pz + pzn, pq + pqn)
            return zn, hzn, pzn, qn, hqn, pqn

        lax.fori_loop(
            first, last, step, (zc, hz, hz0 + hz, qc, hq, hq0 + hq), unroll=UNROLL
        )


def contract(first, second):
    return lax.dot_general(
        first.reshape(-1, MODES),
        second.reshape(-1, MODES),
        (((0,), (0,)), ((), ())),
        preferred_element_type=F32,
    )


def padded(part, rows):
    return jnp.concatenate([part, jnp.zeros((rows - part.shape[0], MODES), F32)], axis=0)


def kernel(
    k_ref, s_ref, modes_hbm, owners_ref, out_ref,
    mid, side, left, right, modes_ref, kb, gb, db, za, qa, zb, qb, s_all, i_all,
    row_in, cor_in, col_i_in, col_s_in, ring_low, s_high, edge_i_in, edge_s_in,
    cor_ring, cor_ring_in, cor_own, partial_out, partial_in, outgoing,
    modes_sem, hsend, hrecv, send, recv, psend, precv, asend, arecv,
):
    rows, cols = lax.axis_size("row"), lax.axis_size("col")
    r, c = lax.axis_index("row"), lax.axis_index("col")
    fetch = pltpu.make_async_copy(modes_hbm, modes_ref, modes_sem)
    fetch.start()
    barrier = pltpu.get_barrier_semaphore()
    others = [neighbour(a, b) for a, b in AROUND] + [neighbour(0, d) for d in range(1, cols)]
    for device in others:
        pl.semaphore_signal(barrier, inc=1, device_id=device, device_id_type=MESH)

    k, s = [
        jnp.concatenate(
            [jnp.zeros((CELLS, 16), F32), ref[...], jnp.zeros((CELLS, 32), F32)], axis=1
        )
        for ref in (k_ref, s_ref)
    ]
    lane = lanes((CELLS, 128))
    mid[0, 16:96, :] = k
    mid[1, 16:96, :] = s
    packed = jnp.where(lane < 64, pltpu.roll(s, 96, 1), 0.0)
    packed = jnp.where(lane < 48, pltpu.roll(k, 80, 1), packed)
    packed = jnp.where(lane < 32, s, packed)
    packed = jnp.where(lane < 16, pltpu.roll(k, 112, 1), packed)
    side[...] = packed
    pl.semaphore_wait(barrier, len(others))
    halo = []
    for n, ((a, b), src, dst) in enumerate(
        (
            ((-1, 0), mid.at[:, 16:32, :], mid.at[:, 96:112, :]),
            ((1, 0), mid.at[:, 80:96, :], mid.at[:, 0:16, :]),
            ((0, -1), side, right.at[16:96, :]),
            ((0, 1), side, left.at[16:96, :]),
            ((-1, -1), side.at[0:16, :], right.at[96:112, :]),
            ((-1, 1), side.at[0:16, :], left.at[96:112, :]),
            ((1, -1), side.at[64:80, :], right.at[0:16, :]),
            ((1, 1), side.at[64:80, :], left.at[0:16, :]),
        )
    ):
        copy = remote(src, dst, hsend.at[n], hrecv.at[n], neighbour(a, b))
        copy.start()
        halo.append(copy)

    omega = omegas()
    scale = 1.0
    for w in omega:
        scale = scale * w / 4.0
    edge = jnp.zeros((8, MODES), F32)
    for ref in (za, qa, zb, qb):
        for line in (0, 1, EXT + 2, EXT + 3):
            ref[line] = jnp.zeros((FRAME, MODES), F32)

    @pl.loop(2, EXT + 2)
    def _(line):
        for ref in (za, qa, zb, qb):
            ref[line, 0:8, :] = edge
            ref[line, 104:112, :] = edge

    cell = lax.broadcasted_iota(jnp.int32, (EXT, MODES), 0)
    first_b, last_b = jnp.where(c == 0, 8, 0), jnp.where(c == cols - 1, 88, EXT)
    weight = jnp.where((cell >= first_b) & (cell < last_b), scale, 0.0)
    fetch.wait()

    def begin(line, carry):
        off = ((r == 0) & (line < 10)) | ((r == rows - 1) & (line >= 90))
        za[line, 8:104, :] = modes_ref[line - 2].astype(F32) * jnp.where(off, 0.0, weight)
        return carry

    lax.fori_loop(2, EXT + 2, begin, 0, unroll=4)

    places = cols * outgoing.shape[2]
    most = outgoing.shape[2] // 8
    lane = lax.broadcasted_iota(jnp.int32, (places, MODES), 1)
    line = lax.broadcasted_iota(jnp.int32, (places, MODES), 0)
    slot = jnp.full((places, MODES), -1, jnp.int32)
    names = [owners_ref[0, g] for g in range(GROUPS)]
    for g in range(GROUPS):
        rank = jnp.int32(0)
        for earlier in range(g):
            rank = rank + (names[earlier] == names[g]).astype(jnp.int32)
        slot = jnp.where(lane // 8 == g, names[g] * most + rank, slot)
    place = ((line // 8 == slot) & (line % 8 == lane % 8)).astype(F32).astype(BF16)

    for copy in halo:
        copy.wait()

    lane = lanes((FRAME, 128))
    line = lax.broadcasted_iota(jnp.int32, (FRAME, 128), 0)
    first_a, last_a = jnp.where(r == 0, 16, 0), jnp.where(r == rows - 1, 96, FRAME)
    first_b, last_b = jnp.where(c == 0, 16, 0), jnp.where(c == cols - 1, 96, FRAME)
    inside = (line >= first_a) & (line < last_a) & (lane >= first_b) & (lane < last_b)
    low, high = left[...], right[...]
    whole = []
    for n, (shift_low, shift_high) in enumerate(((96, 96), (80, 80))):
        x = jnp.where(lane < 96, mid[n], pltpu.roll(high, shift_high, 1))
        x = jnp.where(lane < 16, pltpu.roll(low, shift_low, 1), x)
        whole.append(jnp.where(inside, x, 0.0))
    k, s = whole
    inside = inside.astype(F32)

    def three(x, axis):
        return pltpu.roll(x, 1, axis) + pltpu.roll(x, 127, axis) + 2.0 * x

    total = three(three(padded(k, 128), 0), 1)[:FRAME]
    diagonal = s + 2.0 * k + 0.25 * total
    inverse = inside / (diagonal + (1.0 - inside))
    columns = [padded(x, 128).T[8 : 8 + EXT] for x in (k, inverse, diagonal)]
    for line in range(1, EXT + 3):
        at = line + 6
        kx = jnp.broadcast_to(columns[0][:, at : at + 1], (EXT, MODES))
        kb[line] = kx
        if 2 <= line < EXT + 2:
            gb[line] = jnp.broadcast_to(columns[1][:, at : at + 1], (EXT, MODES))
            db[line] = jnp.broadcast_to(columns[2][:, at : at + 1], (EXT, MODES))
            qa[line, 8:104, :] = kx * za[line, 8:104, :]
        else:
            db[line] = jnp.zeros((EXT, MODES), F32)

    def inner(ref, line, start):
        return ref[line, pl.ds(pl.multiple_of(start - 8, 8), CHUNK), :]

    buffers = ((za, qa), (zb, qb))

    def sweep(t):
        z_to, q_to = buffers[(t + 1) % 2]
        ratio = (1.0 - omega[t]) * 4.0 / omega[t]

        def body(line, start, z, q, u, v):
            kx = inner(kb, line, start)
            new = ratio * z + inner(gb, line, start) * (kx * u + (v - 8.0 * q))
            here = pl.ds(pl.multiple_of(start, 8), CHUNK)
            if t == SWEEPS - 1:
                rounded = new.astype(BF16)
                s_all[line - 2, pl.ds(pl.multiple_of(start - 8, 16), CHUNK), :] = rounded
                new = rounded.astype(F32)
            z_to[line, here, :] = new
            q_to[line, here, :] = kx * new

        return body

    def image(line, start, z, q, u, v):
        value = inner(db, line, start) * z + 2.0 * q - 0.25 * (inner(kb, line, start) * u + v)
        i_all[line - 1, pl.ds(pl.multiple_of(start - 8, 16), CHUNK), :] = value.astype(BF16)

    z_ref, q_ref = buffers[SWEEPS % 2]

    def ring(column, lane, first, last):
        n = last - first
        z = z_ref[first - 1 : last + 1, column, :]
        q = q_ref[first - 1 : last + 1, column, :]
        u = z[0:n] + z[2 : n + 2] + 2.0 * z[1 : n + 1]
        v = q[0:n] + q[2 : n + 2] + 2.0 * q[1 : n + 1]
        return -0.25 * (k[first + 6 : last + 6, lane : lane + 1] * u + v)

    copies = []

    def ship(to, src, dst):
        n = len(copies)
        copy = remote(src, dst, send.at[n], recv.at[n], neighbour(*to))
        copy.start()
        copies.append(copy)

    def ship_columns(image_lines, mode_lines, image_edge, mode_edge, at, edge_at):
        count = image_lines[1] - image_lines[0]
        ship((0, -1), i_all.at[image_lines[0] + 1 : image_lines[1] + 1, 0:16],
             col_i_in.at[at : at + count])
        ship((0, -1), ring_low.at[image_edge : image_edge + 16],
             edge_i_in.at[edge_at : edge_at + 16])
        ship((0, 1), s_all.at[mode_lines[0] : mode_lines[1], 80:96],
             col_s_in.at[at : at + count])
        ship((0, 1), s_high.at[mode_edge : mode_edge + 16],
             edge_s_in.at[edge_at : edge_at + 16])

    done = 0
    start = [2] * SWEEPS + [1]
    for n, stop in enumerate(BLOCKS):
        final = n == len(BLOCKS) - 1
        for t in range(SWEEPS):
            end = stop if final else stop - t
            walk(*buffers[t % 2], start[t], end, sweep(t))
            start[t] = end
        end = EXT + 3 if final else stop - SWEEPS
        walk(z_ref, q_ref, start[SWEEPS], end, image)
        start[SWEEPS] = end
        ready = EXT if final else (end - 2) // 16 * 16
        ring_low[done:ready, :] = ring(8, 7, done + 2, ready + 2).astype(BF16)
        s_high[done:ready, :] = z_ref[done + 2 : ready + 2, 8 + 79, :].astype(BF16)
        done = ready
        if n == 0:
            cor_ring[0] = padded(ring(8, 7, 1, 18), 32).astype(BF16)
            cor_ring[1] = padded(ring(103, 104, 1, 18), 32).astype(BF16)
            ship_columns((0, 8), (8, 16), 0, 0, 0, 0)
            ship((-1, 0), i_all.at[0:17], row_in)
            ship((-1, -1), i_all.at[0:17, 0:16], cor_in.at[0])
            ship((-1, -1), cor_ring.at[0], cor_ring_in.at[0])
            ship((-1, 1), i_all.at[0:17, 80:96], cor_in.at[1])
            ship((-1, 1), cor_ring.at[1], cor_ring_in.at[1])
        elif n == 1:
            ship_columns((16, 32), (32, 48), 16, 32, 8, 16)
        elif n == 2:
            ship_columns((48, 64), (64, 80), 48, 64, 24, 32)
        else:
            ship_columns((80, 96), (80, 96), 80, 80, 40, 48)

    returned = {}

    def give(n, block, to):
        partial_out[n] = block.astype(BF16)
        copy = remote(partial_out.at[n], partial_in.at[n], psend.at[n], precv.at[n], neighbour(*to))
        copy.start()
        returned[n] = copy

    half = lax.broadcasted_iota(jnp.int32, (16, MODES), 0) < 8

    def some(ref, first):
        x = ref[0:16].astype(F32)
        return (jnp.where(half, x, 0.0) if first else jnp.where(half, 0.0, x)).astype(BF16)

    for copy in copies[0:4] + copies[9:17]:
        copy.wait_recv()
    col_lower = contract(s_all[0:8, 80:96], col_i_in[0:8])
    col_lower += contract(s_all[16:32, 80:96], col_i_in[8:24])
    col_lower += contract(s_all[48:64, 80:96], col_i_in[24:40])
    col_lower += contract(some(s_high, True), edge_i_in[0:16])
    col_lower += contract(s_high[16:32], edge_i_in[16:32])
    col_lower += contract(s_high[48:64], edge_i_in[32:48])
    give(0, col_lower, (0, 1))
    col_upper = contract(col_s_in[0:8], i_all[9:17, 0:16])
    col_upper += contract(col_s_in[8:24], i_all[33:49, 0:16])
    col_upper += contract(col_s_in[24:40], i_all[65:81, 0:16])
    col_upper += contract(edge_s_in[0:16], some(ring_low, False))
    col_upper += contract(edge_s_in[16:32], ring_low[32:48])
    col_upper += contract(edge_s_in[32:48], ring_low[64:80])
    give(1, col_upper, (0, -1))
    cor_own[0] = padded(z_ref[81:98, 8 + 79, :], 32).astype(BF16)
    cor_own[1] = padded(z_ref[81:98, 8 + 16, :], 32).astype(BF16)
    for copy in copies[4:9]:
        copy.wait_recv()
    ahead = contract(s_all[79:96, 80:96], cor_in[0]) + contract(cor_own[0], cor_ring_in[0])
    give(2, ahead, (1, 1))
    behind = contract(s_all[79:96, 0:16], cor_in[1]) + contract(cor_own[1], cor_ring_in[1])
    give(3, behind, (1, -1))
    below = contract(s_all[79:96], row_in[...])
    give(4, below, (1, 0))

    def put(slot, block, transposed=False):
        dims = (((1,), (1 if transposed else 0,)), ((), ()))
        rows_out = lax.dot_general(place, block, dims, preferred_element_type=F32)
        outgoing[:, slot] = rows_out.astype(BF16).reshape(cols, -1, MODES)

    def where(a, b, block):
        valid = (r + a >= 0) & (r + a < rows) & (c + b >= 0) & (c + b < cols)
        return jnp.where(valid, block, 0.0).astype(BF16)

    acopies = []

    def scatter(part, first, last):
        out_ref[c, first:last] = outgoing[c, first:last]
        for d in range(1, cols):
            to = neighbour(0, d)
            copy = remote(
                outgoing.at[to[1], first:last],
                out_ref.at[c, first:last],
                asend.at[part, d],
                arecv.at[part, d],
                to,
            )
            copy.start()
            acopies.append(copy)

    total_self = jnp.zeros((MODES, MODES), F32)
    for a in range(0, EXT, 8):
        total_self += contract(s_all[a : a + 8], i_all[a + 1 : a + 9])
    put(0, total_self.astype(BF16))
    put(1, where(1, -1, behind))
    put(2, where(1, 0, below))
    put(3, where(1, 1, ahead))
    scatter(0, 0, 4)
    for copy in copies[17:21]:
        copy.wait_recv()
    late_lower = contract(s_all[80:96, 80:96], col_i_in[40:56])
    late_lower += contract(s_high[80:96], edge_i_in[48:64])
    late_upper = contract(col_s_in[40:56], i_all[81:97, 0:16])
    late_upper += contract(edge_s_in[48:64], ring_low[80:96])
    returned[1].wait_recv()
    put(4, where(0, 1, col_lower + late_lower + partial_in[1].astype(F32)))
    returned[0].wait_recv()
    put(5, where(0, -1, col_upper + late_upper + partial_in[0].astype(F32)), True)
    for n, slot, (a, b) in ((2, 6, (-1, -1)), (3, 8, (-1, 1)), (4, 7, (-1, 0))):
        returned[n].wait_recv()
        put(slot, where(a, b, partial_in[n].astype(F32)), True)
    scatter(1, 4, 9)
    for copy in copies:
        copy.wait_send()
    for copy in returned.values():
        copy.wait_send()
    for copy in acopies:
        copy.wait()


ORDER = (None, 5, 6, 7, 4, 3, 0, 1, 2)


def assemble(conductivity, storage, modes, owners, cols, slots):
    shape = (cols, 9, slots // cols * 8, MODES)
    dma = pltpu.SemaphoreType.DMA

    def bf(*dims):
        return pltpu.VMEM(dims, BF16)

    def f(*dims):
        return pltpu.VMEM(dims, F32)

    return pl.pallas_call(
        kernel,
        out_shape=jax.ShapeDtypeStruct(shape, BF16),
        in_specs=[VMEM, VMEM, pl.BlockSpec(memory_space=pl.ANY), SMEM],
        out_specs=VMEM,
        scratch_shapes=[
            f(2, FRAME, 128), f(CELLS, 128), f(FRAME, 128), f(FRAME, 128), bf(EXT, EXT, MODES),
            *[f(EXT + 4, EXT, MODES)] * 3,
            *[f(EXT + 4, FRAME, MODES)] * 4,
            bf(EXT, EXT, MODES), bf(EXT + 2, EXT, MODES),
            bf(17, EXT, MODES), bf(2, 17, 16, MODES), bf(56, 16, MODES), bf(56, 16, MODES),
            bf(EXT, MODES), bf(EXT, MODES), bf(64, MODES), bf(64, MODES),
            bf(2, 32, MODES), bf(2, 32, MODES), bf(2, 32, MODES),
            bf(5, MODES, MODES), bf(5, MODES, MODES), bf(*shape),
            dma, dma((8,)), dma((8,)), dma((21,)), dma((21,)), dma((5,)), dma((5,)),
            dma((2, cols)), dma((2, cols)),
        ],
        compiler_params=pltpu.CompilerParams(
            collective_id=0, has_side_effects=True, vmem_limit_bytes=60 * 2**20
        ),
    )(conductivity, storage, modes, owners)


def spread_kernel(got_ref, self_ref, cross_ref):
    most = got_ref.shape[2] // 8
    for source in range(got_ref.shape[0]):
        for slot, s in enumerate(ORDER):
            x = got_ref[source, slot].astype(F32)
            for rank in range(most):
                part = x[8 * rank : 8 * rank + 8]
                if s is None:
                    self_ref[0, source * most + rank] = part
                else:
                    cross_ref[0, source * most + rank, s] = part


def spread(got, slots):
    return pl.pallas_call(
        spread_kernel,
        out_shape=(
            jax.ShapeDtypeStruct((1, slots, 8, MODES), F32),
            jax.ShapeDtypeStruct((1, slots, 8, 8, MODES), F32),
        ),
        in_specs=[VMEM],
        out_specs=(VMEM, VMEM),
    )(got)


def on_device(modes, conductivity, storage, owners, slots, cols):
    got = assemble(conductivity, storage, modes, owners.reshape(1, GROUPS), cols, slots)
    return spread(got, slots)


def solution(mesh):
    cols = mesh.shape["col"]
    return jax.shard_map(
        functools.partial(on_device, slots=2 * cols, cols=cols),
        mesh=mesh,
        in_specs=(
            P("row", "col", None),
            P("row", "col"),
            P("row", "col"),
            P("row", "col", None, None),
        ),
        out_specs=(P("row", "col", None, None), P("row", "col", None, None, None)),
        check_vma=False,
    )
```

time: 216 us -> 71.5 us (0.33)
  the two profiles are of different devices: /device:TPU:96 before, /device:TPU:7 now
where the time goes in v2:
time: 71.5 us; the launch traced here: 70.3 us
  Pallas kernels  69.6 us (97%)
    pallas_call x1, Pallas kernels, assemble(): pl.pallas_call(kernel, out_shape=jax.ShapeDtypeStruct(shape, BF16), in_sp...  67.5 us
    pallas_call x1, Pallas kernels, spread(): pl.pallas_call(spread_kernel, out_shape=(jax.ShapeDtypeStruct((1, slots,...  2.15 us

profile of v2, /device:TPU:7, one launch (start us, length us, event | category | flops | bytes accessed | tf_op | source)
XLA Modules:
  0.0 70.3 jit_solution(6392994595122960323)
XLA Ops:
  0.6 67.5 %shard_map.59.got_ref = bf16[16,9,16,128]{3,2,1,0:T(8,128)(2,1)} custom-call(f32[80,80]{1,0:T(8,128)} %k_ref.1, f32[80,80]{1,0:T(8,128)} %s_ref.1, bf16[96,96,128]{2,1,0:T(8,128)(2,1)} %modes_hbm.1, s32[1,16]{1,0:T(1,128)} %bitcast.1), custom_call_target="tpu_custom_call" | custom-call | tf_op jit(solution)/shard_map/pallas_call | solution.py:412
  68.1 2.2 %shard_map.60 = (f32[1,32,8,128]{3,2,1,0:T(8,128)}, f32[1,32,8,8,128]{4,3,2,1,0:T(8,128)}) custom-call(bf16[16,9,16,128]{3,2,1,0:T(8,128)(2,1)} %shard_map.59.got_ref), custom_call_target="tpu_custom_call" | custom-call | tf_op jit(solution)/shard_map/pallas_call | solution.py:449

commit v3 on v2

--- a/solution.py
+++ b/solution.py
@@ -14,14 +14,23 @@
 SWEEPS = 3
 GROUPS = 16
 FRAME = 112
-CHUNK = 32
+CHUNK = 48
 MESH = pl.DeviceIdType.MESH
 F32 = jnp.float32
 BF16 = jnp.bfloat16
 VMEM = pl.BlockSpec(memory_space=pltpu.VMEM)
 SMEM = pl.BlockSpec(memory_space=pltpu.SMEM)
-BLOCKS = (22, 54, 86, 98)
-UNROLL = 8
+BLOCKS = (
+    ((2, 22), (2, 21), (2, 20), (1, 19)),
+    ((79, 98), (80, 98), (81, 98), (82, 99)),
+    ((22, 46), (21, 45), (20, 44), (19, 43)),
+    ((46, 70), (45, 69), (44, 68), (43, 67)),
+    ((70, 79), (69, 80), (68, 81), (67, 82)),
+)
+SPREAD = ((1, 23), (78, 99), (23, 47), (47, 71), (71, 78))
+EDGES = ((0, 16), (80, 96), (16, 32), (32, 64), (64, 80))
+UNROLL = 12
+PLANE = 4
 
 
 def neighbour(da, db):
@@ -95,8 +104,8 @@
     k_ref, s_ref, modes_hbm, owners_ref, out_ref,
     mid, side, left, right, modes_ref, kb, gb, db, za, qa, zb, qb, s_all, i_all,
     row_in, cor_in, col_i_in, col_s_in, ring_low, s_high, edge_i_in, edge_s_in,
-    cor_ring, cor_ring_in, cor_own, partial_out, partial_in, outgoing,
-    modes_sem, hsend, hrecv, send, recv, psend, precv, asend, arecv,
+    cor_ring, cor_ring_in, cor_own, partial_out, partial_in, outgoing, relay,
+    modes_sem, hsend, hrecv, send, recv, psend, precv, asend, arecv, csend, crecv, rrecv, fsend,
 ):
     rows, cols = lax.axis_size("row"), lax.axis_size("col")
     r, c = lax.axis_index("row"), lax.axis_index("col")
@@ -203,16 +212,17 @@
     diagonal = s + 2.0 * k + 0.25 * total
     inverse = inside / (diagonal + (1.0 - inside))
     columns = [padded(x, 128).T[8 : 8 + EXT] for x in (k, inverse, diagonal)]
-    for line in range(1, EXT + 3):
-        at = line + 6
-        kx = jnp.broadcast_to(columns[0][:, at : at + 1], (EXT, MODES))
-        kb[line] = kx
-        if 2 <= line < EXT + 2:
-            gb[line] = jnp.broadcast_to(columns[1][:, at : at + 1], (EXT, MODES))
-            db[line] = jnp.broadcast_to(columns[2][:, at : at + 1], (EXT, MODES))
-            qa[line, 8:104, :] = kx * za[line, 8:104, :]
-        else:
-            db[line] = jnp.zeros((EXT, MODES), F32)
+    def spread_lines(first, last):
+        for line in range(first, last):
+            at = line + 6
+            kx = jnp.broadcast_to(columns[0][:, at : at + 1], (EXT, MODES))
+            kb[line] = kx
+            if 2 <= line < EXT + 2:
+                gb[line] = jnp.broadcast_to(columns[1][:, at : at + 1], (EXT, MODES))
+                db[line] = jnp.broadcast_to(columns[2][:, at : at + 1], (EXT, MODES))
+                qa[line, 8:104, :] = kx * za[line, 8:104, :]
+            else:
+                db[line] = jnp.zeros((EXT, MODES), F32)
 
     def inner(ref, line, start):
         return ref[line, pl.ds(pl.multiple_of(start - 8, 8), CHUNK), :]
@@ -258,47 +268,91 @@
         copy.start()
         copies.append(copy)
 
-    def ship_columns(image_lines, mode_lines, image_edge, mode_edge, at, edge_at):
-        count = image_lines[1] - image_lines[0]
-        ship((0, -1), i_all.at[image_lines[0] + 1 : image_lines[1] + 1, 0:16],
-             col_i_in.at[at : at + count])
-        ship((0, -1), ring_low.at[image_edge : image_edge + 16],
-             edge_i_in.at[edge_at : edge_at + 16])
-        ship((0, 1), s_all.at[mode_lines[0] : mode_lines[1], 80:96],
-             col_s_in.at[at : at + count])
-        ship((0, 1), s_high.at[mode_edge : mode_edge + 16],
-             edge_s_in.at[edge_at : edge_at + 16])
-
-    done = 0
-    start = [2] * SWEEPS + [1]
-    for n, stop in enumerate(BLOCKS):
-        final = n == len(BLOCKS) - 1
-        for t in range(SWEEPS):
-            end = stop if final else stop - t
-            walk(*buffers[t % 2], start[t], end, sweep(t))
-            start[t] = end
-        end = EXT + 3 if final else stop - SWEEPS
-        walk(z_ref, q_ref, start[SWEEPS], end, image)
-        start[SWEEPS] = end
-        ready = EXT if final else (end - 2) // 16 * 16
-        ring_low[done:ready, :] = ring(8, 7, done + 2, ready + 2).astype(BF16)
-        s_high[done:ready, :] = z_ref[done + 2 : ready + 2, 8 + 79, :].astype(BF16)
-        done = ready
-        if n == 0:
-            cor_ring[0] = padded(ring(8, 7, 1, 18), 32).astype(BF16)
-            cor_ring[1] = padded(ring(103, 104, 1, 18), 32).astype(BF16)
-            ship_columns((0, 8), (8, 16), 0, 0, 0, 0)
-            ship((-1, 0), i_all.at[0:17], row_in)
-            ship((-1, -1), i_all.at[0:17, 0:16], cor_in.at[0])
-            ship((-1, -1), cor_ring.at[0], cor_ring_in.at[0])
-            ship((-1, 1), i_all.at[0:17, 80:96], cor_in.at[1])
-            ship((-1, 1), cor_ring.at[1], cor_ring_in.at[1])
-        elif n == 1:
-            ship_columns((16, 32), (32, 48), 16, 32, 8, 16)
-        elif n == 2:
-            ship_columns((48, 64), (64, 80), 48, 64, 24, 32)
+    def ship_edges(at, image_edge, mode_edge):
+        ship((0, -1), ring_low.at[image_edge : image_edge + 16], edge_i_in.at[at : at + 16])
+        ship((0, 1), s_high.at[mode_edge : mode_edge + 16], edge_s_in.at[at : at + 16])
+
+    x = lax.rem(c, PLANE)
+    ways = (
+        (i_all, lambda lines: (lines[0] + 1, 0), col_i_in, -1, 0, PLANE - 1),
+        (s_all, lambda lines: (lines[0], 80), col_s_in, 1, PLANE - 1, 0),
+    )
+    pieces = (
+        (((0, 8), (8, 16)), 0),
+        (((80, 88), (88, 96)), 8),
+        (((16, 24), (24, 32)), 16),
+    )
+
+    def strip(n, w, quarter=None, to=None):
+        source, place_of, target, sign, _, _ = ways[w]
+        lines, at = pieces[n]
+        first, column = place_of(lines[w])
+        count = lines[w][1] - lines[w][0]
+        if quarter is None:
+            quarter, size = 0, count
         else:
-            ship_columns((80, 96), (80, 96), 80, 80, 40, 48)
+            size = count // PLANE
+        src = source.at[pl.ds(first + quarter * size, size), column : column + 16]
+        if to is None:
+            return remote(src, target.at[pl.ds(at + quarter * size, size)], csend.at[n, w, quarter],
+                          crecv.at[n, w, quarter], neighbour(0, sign))
+        return remote(src, relay.at[n, w, 0:size], csend.at[n, w, quarter], rrecv.at[n, w],
+                      neighbour(0, to))
+
+    def onward(n, w):
+        _, _, target, sign, _, _ = ways[w]
+        lines, at = pieces[n]
+        size = (lines[w][1] - lines[w][0]) // PLANE
+        quarter = x if sign < 0 else PLANE - 1 - x
+        return remote(relay.at[n, w, 0:size], target.at[pl.ds(at + quarter * size, size)],
+                      fsend.at[n, w], crecv.at[n, w, quarter],
+                      neighbour(0, sign * (1 + quarter)))
+
+    def ship_columns(n):
+        for w, (_, _, _, sign, sender, _) in enumerate(ways):
+
+            @pl.when(x != sender)
+            def _(n=n, w=w):
+                strip(n, w).start()
+
+            @pl.when(x == sender)
+            def _(n=n, w=w, sign=sign):
+                strip(n, w, 0).start()
+                for q in range(1, PLANE):
+                    strip(n, w, q, -sign * q).start()
+
+    def pass_on(n):
+        for w, (_, _, _, _, sender, _) in enumerate(ways):
+
+            @pl.when(x != sender)
+            def _(n=n, w=w):
+                strip(n, w, 0, 1).wait_recv()
+                onward(n, w).start()
+
+    def columns_arrived(n):
+        for w, (_, _, _, _, _, receiver) in enumerate(ways):
+
+            @pl.when(x != receiver)
+            def _(n=n, w=w):
+                strip(n, w).wait_recv()
+
+            @pl.when(x == receiver)
+            def _(n=n, w=w):
+                for q in range(PLANE):
+                    strip(n, w, q).wait_recv()
+
+    def columns_left(n):
+        for w, (_, _, _, _, sender, _) in enumerate(ways):
+
+            @pl.when(x != sender)
+            def _(n=n, w=w):
+                strip(n, w).wait_send()
+                onward(n, w).wait_send()
+
+            @pl.when(x == sender)
+            def _(n=n, w=w):
+                for q in range(PLANE):
+                    strip(n, w, q).wait_send()
 
     returned = {}
 
@@ -307,39 +361,6 @@
         copy = remote(partial_out.at[n], partial_in.at[n], psend.at[n], precv.at[n], neighbour(*to))
         copy.start()
         returned[n] = copy
-
-    half = lax.broadcasted_iota(jnp.int32, (16, MODES), 0) < 8
-
-    def some(ref, first):
-        x = ref[0:16].astype(F32)
-        return (jnp.where(half, x, 0.0) if first else jnp.where(half, 0.0, x)).astype(BF16)
-
-    for copy in copies[0:4] + copies[9:17]:
-        copy.wait_recv()
-    col_lower = contract(s_all[0:8, 80:96], col_i_in[0:8])
-    col_lower += contract(s_all[16:32, 80:96], col_i_in[8:24])
-    col_lower += contract(s_all[48:64, 80:96], col_i_in[24:40])
-    col_lower += contract(some(s_high, True), edge_i_in[0:16])
-    col_lower += contract(s_high[16:32], edge_i_in[16:32])
-    col_lower += contract(s_high[48:64], edge_i_in[32:48])
-    give(0, col_lower, (0, 1))
-    col_upper = contract(col_s_in[0:8], i_all[9:17, 0:16])
-    col_upper += contract(col_s_in[8:24], i_all[33:49, 0:16])
-    col_upper += contract(col_s_in[24:40], i_all[65:81, 0:16])
-    col_upper += contract(edge_s_in[0:16], some(ring_low, False))
-    col_upper += contract(edge_s_in[16:32], ring_low[32:48])
-    col_upper += contract(edge_s_in[32:48], ring_low[64:80])
-    give(1, col_upper, (0, -1))
-    cor_own[0] = padded(z_ref[81:98, 8 + 79, :], 32).astype(BF16)
-    cor_own[1] = padded(z_ref[81:98, 8 + 16, :], 32).astype(BF16)
-    for copy in copies[4:9]:
-        copy.wait_recv()
-    ahead = contract(s_all[79:96, 80:96], cor_in[0]) + contract(cor_own[0], cor_ring_in[0])
-    give(2, ahead, (1, 1))
-    behind = contract(s_all[79:96, 0:16], cor_in[1]) + contract(cor_own[1], cor_ring_in[1])
-    give(3, behind, (1, -1))
-    below = contract(s_all[79:96], row_in[...])
-    give(4, below, (1, 0))
 
     def put(slot, block, transposed=False):
         dims = (((1,), (1 if transposed else 0,)), ((), ()))
@@ -366,28 +387,109 @@
             copy.start()
             acopies.append(copy)
 
+    for n, (block, (spread_first, spread_last), (edge_first, edge_last)) in enumerate(
+        zip(BLOCKS, SPREAD, EDGES, strict=True)
+    ):
+        spread_lines(spread_first, spread_last)
+        for t in range(SWEEPS):
+            walk(*buffers[t % 2], *block[t], sweep(t))
+        walk(z_ref, q_ref, *block[SWEEPS], image)
+        first, last = edge_first + 2, edge_last + 2
+        ring_low[edge_first:edge_last, :] = ring(8, 7, first, last).astype(BF16)
+        s_high[edge_first:edge_last, :] = z_ref[first:last, 8 + 79, :].astype(BF16)
+        if n == 0:
+            cor_ring[0] = padded(ring(8, 7, 1, 18), 32).astype(BF16)
+            cor_ring[1] = padded(ring(103, 104, 1, 18), 32).astype(BF16)
+            ship((-1, 0), i_all.at[0:17], row_in)
+            ship((-1, -1), i_all.at[0:17, 0:16], cor_in.at[0])
+            ship((-1, -1), cor_ring.at[0], cor_ring_in.at[0])
+            ship((-1, 1), i_all.at[0:17, 80:96], cor_in.at[1])
+            ship((-1, 1), cor_ring.at[1], cor_ring_in.at[1])
+            ship_columns(0)
+            ship_edges(0, 0, 0)
+        elif n == 1:
+            ship_columns(1)
+            ship_edges(16, 80, 80)
+            pass_on(0)
+            cor_own[0] = padded(z_ref[81:98, 8 + 79, :], 32).astype(BF16)
+            cor_own[1] = padded(z_ref[81:98, 8 + 16, :], 32).astype(BF16)
+        elif n == 2:
+            ship_columns(2)
+            ship_edges(32, 16, 16)
+            pass_on(1)
+        elif n == 3:
+            ship((0, -1), i_all.at[33:49, 0:16], col_i_in.at[24:40])
+            ship((0, 1), s_all.at[48:64, 80:96], col_s_in.at[24:40])
+            ship_edges(48, 32, 48)
+            pass_on(2)
+        else:
+            ship((0, -1), i_all.at[65:81, 0:16], col_i_in.at[40:56])
+            ship((0, 1), s_all.at[64:80, 80:96], col_s_in.at[40:56])
+            ship_edges(64, 64, 64)
+            for copy in copies[0:5]:
+                copy.wait_recv()
+            ahead = contract(s_all[79:96, 80:96], cor_in[0])
+            ahead += contract(cor_own[0], cor_ring_in[0])
+            give(2, ahead, (1, 1))
+            behind = contract(s_all[79:96, 0:16], cor_in[1])
+            behind += contract(cor_own[1], cor_ring_in[1])
+            give(3, behind, (1, -1))
+            below = contract(s_all[79:96], row_in[...])
+            give(4, below, (1, 0))
+            put(0, where(1, -1, behind))
+            put(1, where(1, 0, below))
+            put(2, where(1, 1, ahead))
+
+    half = lax.broadcasted_iota(jnp.int32, (16, MODES), 0) < 8
+
+    def some(part, first):
+        x = part.astype(F32)
+        return (jnp.where(half, x, 0.0) if first else jnp.where(half, 0.0, x)).astype(BF16)
+
+    for n in range(3):
+        columns_arrived(n)
+    for copy in copies[5:15]:
+        copy.wait_recv()
+    col_lower = contract(s_all[0:8, 80:96], col_i_in[0:8])
+    col_lower += contract(s_all[80:88, 80:96], col_i_in[8:16])
+    col_lower += contract(s_all[16:24, 80:96], col_i_in[16:24])
+    col_lower += contract(s_all[32:48, 80:96], col_i_in[24:40])
+    col_lower += contract(some(s_high[0:16], True), edge_i_in[0:16])
+    col_lower += contract(some(s_high[80:96], True), edge_i_in[16:32])
+    col_lower += contract(some(s_high[16:32], True), edge_i_in[32:48])
+    col_lower += contract(s_high[32:48], edge_i_in[48:64])
+    give(0, col_lower, (0, 1))
+    col_upper = contract(col_s_in[0:8], i_all[9:17, 0:16])
+    col_upper += contract(col_s_in[8:16], i_all[89:97, 0:16])
+    col_upper += contract(col_s_in[16:24], i_all[25:33, 0:16])
+    col_upper += contract(col_s_in[24:40], i_all[49:65, 0:16])
+    col_upper += contract(edge_s_in[0:16], some(ring_low[0:16], False))
+    col_upper += contract(edge_s_in[16:32], some(ring_low[80:96], False))
+    col_upper += contract(edge_s_in[32:48], some(ring_low[16:32], False))
+    col_upper += contract(edge_s_in[48:64], ring_low[48:64])
+    give(1, col_upper, (0, -1))
+    scatter(0, 0, 3)
+    for n, slot, (a, b) in ((2, 4, (-1, -1)), (4, 5, (-1, 0)), (3, 6, (-1, 1))):
+        returned[n].wait_recv()
+        put(slot, where(a, b, partial_in[n].astype(F32)), True)
     total_self = jnp.zeros((MODES, MODES), F32)
     for a in range(0, EXT, 8):
         total_self += contract(s_all[a : a + 8], i_all[a + 1 : a + 9])
-    put(0, total_self.astype(BF16))
-    put(1, where(1, -1, behind))
-    put(2, where(1, 0, below))
-    put(3, where(1, 1, ahead))
-    scatter(0, 0, 4)
-    for copy in copies[17:21]:
+    put(3, total_self.astype(BF16))
+    scatter(1, 3, 7)
+    for copy in copies[15:19]:
         copy.wait_recv()
-    late_lower = contract(s_all[80:96, 80:96], col_i_in[40:56])
-    late_lower += contract(s_high[80:96], edge_i_in[48:64])
-    late_upper = contract(col_s_in[40:56], i_all[81:97, 0:16])
-    late_upper += contract(edge_s_in[48:64], ring_low[80:96])
+    late_lower = contract(s_all[64:80, 80:96], col_i_in[40:56])
+    late_lower += contract(s_high[64:80], edge_i_in[64:80])
+    late_upper = contract(col_s_in[40:56], i_all[65:81, 0:16])
+    late_upper += contract(edge_s_in[64:80], ring_low[64:80])
     returned[1].wait_recv()
-    put(4, where(0, 1, col_lower + late_lower + partial_in[1].astype(F32)))
+    put(7, where(0, 1, col_lower + late_lower + partial_in[1].astype(F32)))
     returned[0].wait_recv()
-    put(5, where(0, -1, col_upper + late_upper + partial_in[0].astype(F32)), True)
-    for n, slot, (a, b) in ((2, 6, (-1, -1)), (3, 8, (-1, 1)), (4, 7, (-1, 0))):
-        returned[n].wait_recv()
-        put(slot, where(a, b, partial_in[n].astype(F32)), True)
-    scatter(1, 4, 9)
+    put(8, where(0, -1, col_upper + late_upper + partial_in[0].astype(F32)), True)
+    scatter(2, 7, 9)
+    for n in range(3):
+        columns_left(n)
     for copy in copies:
         copy.wait_send()
     for copy in returned.values():
@@ -396,7 +498,7 @@
         copy.wait()
 
 
-ORDER = (None, 5, 6, 7, 4, 3, 0, 1, 2)
+ORDER = (5, 6, 7, None, 0, 1, 2, 4, 3)
 
 
 def assemble(conductivity, storage, modes, owners, cols, slots):
@@ -420,11 +522,12 @@
             *[f(EXT + 4, FRAME, MODES)] * 4,
             bf(EXT, EXT, MODES), bf(EXT + 2, EXT, MODES),
             bf(17, EXT, MODES), bf(2, 17, 16, MODES), bf(56, 16, MODES), bf(56, 16, MODES),
-            bf(EXT, MODES), bf(EXT, MODES), bf(64, MODES), bf(64, MODES),
+            bf(EXT, MODES), bf(EXT, MODES), bf(80, MODES), bf(80, MODES),
             bf(2, 32, MODES), bf(2, 32, MODES), bf(2, 32, MODES),
-            bf(5, MODES, MODES), bf(5, MODES, MODES), bf(*shape),
-            dma, dma((8,)), dma((8,)), dma((21,)), dma((21,)), dma((5,)), dma((5,)),
-            dma((2, cols)), dma((2, cols)),
+            bf(5, MODES, MODES), bf(5, MODES, MODES), bf(*shape), bf(3, 2, 2, 16, MODES),
+            dma, dma((8,)), dma((8,)), dma((19,)), dma((19,)), dma((5,)), dma((5,)),
+            dma((3, cols)), dma((3, cols)),
+            dma((3, 2, PLANE)), dma((3, 2, PLANE)), dma((3, 2)), dma((3, 2)),
         ],
         compiler_params=pltpu.CompilerParams(
             collective_id=0, has_side_effects=True, vmem_limit_bytes=60 * 2**20

time: 71.5 us -> 69.3 us (0.969)
  Pallas kernels: 69.6 us -> 67.3 us
    pallas_call x1, Pallas kernels: 67.5 us -> 65.1 us  [assemble(): pl.pallas_call(kernel, out_shape=jax.ShapeDtypeStruct(shape, BF16), in_sp...]
where the time goes in v3:
time: 69.3 us; the launch traced here: 67.9 us
  Pallas kernels  67.3 us (97%)
    pallas_call x1, Pallas kernels, assemble(): pl.pallas_call(kernel, out_shape=jax.ShapeDtypeStruct(shape, BF16), in_sp...  65.1 us
    pallas_call x1, Pallas kernels, spread(): pl.pallas_call(spread_kernel, out_shape=(jax.ShapeDtypeStruct((1, slots,...  2.15 us

profile of v3, /device:TPU:7, one launch (start us, length us, event | category | flops | bytes accessed | tf_op | source)
XLA Modules:
  0.0 67.9 jit_solution(5326338757070604970)
XLA Ops:
  0.6 65.1 %shard_map.59.got_ref = bf16[16,9,16,128]{3,2,1,0:T(8,128)(2,1)} custom-call(f32[80,80]{1,0:T(8,128)} %k_ref.1, f32[80,80]{1,0:T(8,128)} %s_ref.1, bf16[96,96,128]{2,1,0:T(8,128)(2,1)} %modes_hbm.1, s32[1,16]{1,0:T(1,128)} %bitcast.1), custom_call_target="tpu_custom_call" | custom-call | tf_op jit(solution)/shard_map/pallas_call | solution.py:514
  65.8 2.2 %shard_map.60 = (f32[1,32,8,128]{3,2,1,0:T(8,128)}, f32[1,32,8,8,128]{4,3,2,1,0:T(8,128)}) custom-call(bf16[16,9,16,128]{3,2,1,0:T(8,128)(2,1)} %shard_map.59.got_ref), custom_call_target="tpu_custom_call" | custom-call | tf_op jit(solution)/shard_map/pallas_call | solution.py:552
